TPU v7x, 512 devices: a whole 4x4x16 slice. The times are simulated.
512 devices in a mesh: dp: 64 (over z, y_lo, core), tensor: 8 (over y_hi, x).
Axes of the slice: x: 4, y: 4 (y_hi: 2, y_lo: 2; y = y_hi * 2 + y_lo), z: 16, core: 2. Of those that a mesh axis runs over, the one named last changes fastest.
Arguments:
- pooled: bfloat16 [16384, 1792], P(('dp', 'tensor')), as said below
- texts: bfloat16 [16384, 1792], P(('dp', 'tensor')), as said below
- head_w: bfloat16 [1792, 1792], P('tensor'), may hold values from -0.125 to 0.125
- log_scale: float32 [1], replicated, may hold values from 2.3 to 3.4
- bias: float32 [1], replicated, may hold values from -4 to -1
Outputs:
- grad_pooled: float32 [16384, 1792], P(('dp', 'tensor'))
- grad_head: float32 [1792, 1792], P('dp', 'tensor')
Inputs may be any that keep to these rules, and one draw needn't show every extreme that they name: `pooled`: finite real values. `texts`: finite real values, no row zero.
All inputs are finite; a program needn't handle non-finite values.
Results may differ from a plain program's by a relative error of at most 0.025.
Values may be sent and summed in bfloat16 or wider, within the bound.
No kernel may reach another device: no remote copies, remote signals or barrier semaphores. Data moves between devices by JAX's collectives and lax.ppermute only.
A program may use at most 64 MiB of HBM per device.

v0:
```python
import jax
import jax.numpy as jnp
from jax import lax
from jax.sharding import PartitionSpec as P


def per_device(pooled, texts, head_w, log_scale, bias):
    tensor_index = lax.axis_index("tensor")
    batch_index = lax.axis_index("dp")
    image_rows = lax.all_gather(pooled, "tensor", axis=0, tiled=True)
    shard_count = image_rows.shape[0]
    text_count = texts.shape[0]
    col_count = head_w.shape[0]
    projected_cols = lax.dot_general(
        image_rows, head_w, (((1,), (1,)), ((), ())), preferred_element_type=jnp.float32
    ).astype(jnp.bfloat16)
    projected = lax.all_gather(projected_cols, "tensor", axis=1, tiled=True)
    proj_float = projected.astype(jnp.float32)
    row_norms = jnp.sqrt(jnp.sum(proj_float * proj_float, axis=1, keepdims=True) + 1e-06)
    unit_rows = proj_float / row_norms
    embedded = unit_rows.astype(jnp.bfloat16)
    text_float = texts.astype(jnp.float32)
    text_unit = (
        text_float / jnp.sqrt(jnp.sum(text_float * text_float, axis=1, keepdims=True) + 1e-06)
    ).astype(jnp.bfloat16)
    logit_scale = jnp.exp(log_scale[0])
    logit_bias = bias[0]
    image_ids = batch_index * shard_count + jnp.arange(shard_count, dtype=jnp.int32)
    text_block = lax.all_gather(text_unit, "dp", axis=0, tiled=True)
    positions = jnp.arange(text_block.shape[0], dtype=jnp.int32)
    text_ids = (
        positions // text_count * shard_count + tensor_index * text_count + positions % text_count
    )
    scores = lax.dot_general(
        embedded, text_block, (((1,), (1,)), ((), ())), preferred_element_type=jnp.float32
    )
    logits = logit_scale * scores + logit_bias
    labels = jnp.where(image_ids[:, None] == text_ids[None, :], 1.0, -1.0).astype(jnp.float32)
    pair_grad = (-labels * jax.nn.sigmoid(-labels * logits)).astype(jnp.bfloat16)
    text_terms = jnp.dot(pair_grad, text_block, preferred_element_type=jnp.float32)
    col_start = tensor_index * col_count
    grad_embed = logit_scale * lax.psum(text_terms.astype(jnp.bfloat16), "tensor").astype(
        jnp.float32
    )
    row_dots = jnp.sum(unit_rows * grad_embed, axis=1, keepdims=True)
    grad_full = (grad_embed - unit_rows * row_dots) / row_norms
    grad_cols = lax.dynamic_slice_in_dim(grad_full, col_start, col_count, 1)
    grad_proj = grad_cols.astype(jnp.bfloat16)
    grad_pooled = lax.psum_scatter(
        jnp.dot(grad_proj, head_w, preferred_element_type=jnp.float32).astype(jnp.bfloat16),
        "tensor",
        scatter_dimension=0,
        tiled=True,
    ).astype(jnp.float32)
    grad_head = lax.psum_scatter(
        lax.dot_general(
            image_rows, grad_proj, (((0,), (0,)), ((), ())), preferred_element_type=jnp.float32
        ),
        "dp",
        scatter_dimension=0,
        tiled=True,
    )
    return (grad_pooled, grad_head)


def solution(mesh):
    in_specs = (P(("dp", "tensor"), None), P(("dp", "tensor"), None), P("tensor", None), P(), P())
    out_specs = (P(("dp", "tensor"), None), P("dp", "tensor"))
    return jax.shard_map(
        per_device, mesh=mesh, in_specs=in_specs, out_specs=out_specs, check_vma=False
    )
```

profile of v0, /device:TPU:24, one launch (start us, length us, event | category | flops | bytes accessed | tf_op | source)
XLA Modules:
  0.0 781.3 jit_solution(875045438825275835)
XLA Ops:
  7.2 0.0 copy-start
  7.2 0.0 all-gather.2.cloned.1.call-start
  7.2 1.1 fusion.11
  8.3 1.6 fusion.12
  10.0 0.0 all-gather.2.cloned.1.call-update
  10.0 0.0 all-reduce.4.cloned.1.call-start
  11.4 36.5 %all_gather.9 = bf16[256,1792]{1,0:T(8,128)(2,1)S(1)} all-gather(bf16[32,1792]{1,0:T(8,128)(2,1)} %param.5), channel_id=1, replica_groups=mesh['dp'=64,'tensor'=8] {'tensor'}, dimensions={0}, use_global_device_ids=true | all-gather | bytes 1032192 | tf_op jit(solution)/shard_map/all_gather | solution.py:10
  47.9 0.0 copy-done
  47.9 0.5 convolution_convert_fusion.2
  48.3 36.2 %all_gather.10 = bf16[256,1792]{0,1:T(8,128)(2,1)S(1)} all-gather(bf16[256,224]{0,1:T(8,128)(2,1)S(1)} %convolution_convert_fusion.2), channel_id=1, replica_groups=mesh['dp'=64,'tensor'=8] {'tensor'}, dimensions={1}, use_global_device_ids=true | all-gather | bytes 1032192 | tf_op jit(solution)/shard_map/all_gather | solution.py:17
  84.5 0.3 fusion.8
  84.8 58.1 %all-gather.2.cloned.1.call-done = bf16[2048,1792]{1,0:T(8,128)(2,1)} async-done(((bf16[32,1792]{1,0:T(8,128)(2,1)}), bf16[2048,1792]{1,0:T(8,128)(2,1)}) %all-gather.2.cloned.1.call-update) | async-done | bytes 7340048 | tf_op jit(solution)/shard_map/all_gather | solution.py:29
  143.0 11.2 %convolution_convert_fusion = bf16[256,1792]{0,1:T(8,128)(2,1)} fusion(bf16[2048,1792]{1,0:T(8,128)(2,1)} %all-gather.2.cloned.1.call-done, f32[]{:T(128)} %bitcast.13, f32[]{:T(128)} %bitcast, s32[2048]{0:T(1024)S(1)} %fusion.23, s32[256]{0:T(256)S(1)} %iota_add_fusion, bf16[256,1792]{0,1:T(8,128)(2,1)S(1)} %all_gather.10, f32[256]{0:T(256)S(1)} %add_sqrt_fusion), kind=kOutput, calls=%fused_computation.10 | convolution fusion | flops 3765698560 | bytes 9185288 | tf_op jit(solution)/shard_map/dot_general | solution.py:40
  154.2 0.0 all-reduce.4.cloned.1.call-update
  154.2 0.0 all-reduce.6.cloned.1.call-start
  154.2 97.1 %all-reduce.4.cloned.1.call-done = bf16[256,1792]{0,1:T(8,128)(2,1)} async-done(((bf16[256,1792]{0,1:T(8,128)(2,1)}), bf16[256,1792]{0,1:T(8,128)(2,1)}) %all-reduce.4.cloned.1.call-update) | async-done | bytes 917520 | tf_op jit(solution)/shard_map/psum | solution.py:42
  251.3 1.6 multiply_reduce_fusion
  252.9 0.0 copy-start.1
  252.9 0.0 copy-start.2
  252.9 1.2 copy-done.1
  254.2 0.6 copy-done.2
  254.7 1.6 convolution_bitcast_fusion
  256.4 0.0 all-reduce.6.cloned.1.call-update
  256.4 0.0 reduce-scatter.3.cloned.1.call-start
  256.4 2.4 convolution_convert_fusion.1
  258.9 0.0 reduce-scatter.3.cloned.1.call-update
  258.9 1.3 dynamic-slice
  260.8 418.6 %all-reduce.6.cloned.1.call-done = f32[1792,224]{0,1:T(8,128)} async-done(((f32[1792,224]{0,1:T(8,128)}), f32[1792,224]{0,1:T(8,128)}) %all-reduce.6.cloned.1.call-update) | async-done | bytes 1605648
  679.4 1.0 constant_dynamic-slice_fusion
  680.4 0.7 copy.10
  681.1 92.0 %reduce-scatter.3.cloned.1.call-done = bf16[32,1792]{1,0:T(8,128)(2,1)} async-done(((bf16[256,1792]{1,0:T(8,128)(2,1)}), bf16[32,1792]{1,0:T(8,128)(2,1)}) %reduce-scatter.3.cloned.1.call-update) | async-done | bytes 114704 | tf_op jit(solution)/shard_map/reduce_scatter | solution.py:49
  773.1 1.6 convert_element_type.43
  (4 shorter events, 0.0 us)
Async XLA Ops:
  7.2 40.7 %copy-start = (bf16[224,1792]{1,0:T(8,128)(2,1)S(1)}, bf16[224,1792]{1,0:T(8,128)(2,1)}, u32[]{:S(2)}) copy-start(bf16[224,1792]{1,0:T(8,128)(2,1)} %param.7) | copy-start | bytes 2408452
  7.2 135.8 %all-gather.2.cloned.1.call-start = ((), (), s32[]{:S(2)}) async-start(), calls=%async_computation.1 | async-start | bytes 7454720 | tf_op jit(solution)/shard_map/all_gather | solution.py:29
  10.0 241.3 %all-reduce.4.cloned.1.call-start = ((), (), s32[]{:S(2)}) async-start(), calls=%async_computation.2 | async-start | bytes 1835008 | tf_op jit(solution)/shard_map/psum | solution.py:42
  154.2 525.2 %all-reduce.6.cloned.1.call-start = ((), (), s32[]{:S(2)}) async-start(), calls=%async_computation.4 | async-start | bytes 3211264
  252.9 1.2 copy-start.1
  252.9 1.8 copy-start.2
  256.4 516.8 %reduce-scatter.3.cloned.1.call-start = ((), (), s32[]{:S(2)}) async-start(), calls=%async_computation.3 | async-start | bytes 1032192 | tf_op jit(solution)/shard_map/reduce_scatter | solution.py:49
Sparse Core Ops, SparseCore 0:
  10.7 132.1 all-gather.1
  154.3 96.9 all-reduce.3
  256.5 422.8 all-reduce.5
  683.8 89.3 reduce-scatter.2
where the time goes:
time: 782 us; the launch traced here: 781 us
  waiting for transfers between devices  666 us (85%)
  blocking collectives  72.7 us (9%)
  between operations  15.8 us (2%)
  matrix products  15.7 us (2%)
    unnamed x5, waiting for transfers between devices  419 us
    psum x1, waiting for transfers between devices, per_device(): lax.psum(text_terms.astype(jnp.bfloat16), 'tensor').astype(jnp.float32)  97.1 us
    reduce_scatter x1, waiting for transfers between devices, per_device(): lax.psum_scatter(jnp.dot(grad_proj, head_w, preferred_element_type=jnp.fl...  92 us
    all_gather x1, waiting for transfers between devices, per_device(): text_block = lax.all_gather(text_unit, 'dp', axis=0, tiled=True)  58.1 us
    all_gather x1, blocking collectives, per_device(): image_rows = lax.all_gather(pooled, 'tensor', axis=0, tiled=True)  36.5 us
    all_gather x1, blocking collectives, per_device(): projected = lax.all_gather(projected_cols, 'tensor', axis=1, tiled=True)  36.2 us
  transfers between devices with their start and end apart: 4, of which 4 were waited for; matrix products, arithmetic and copies ran while one was open for 1% of the time, Pallas kernels for 0%

commit v1 on v0

v1 whole, which is shorter than its diff:
```python
import jax
import jax.numpy as jnp
from jax import lax
from jax.sharding import Mesh, PartitionSpec as P

BF = jnp.bfloat16
F32 = jnp.float32
T = ("yh", "x")
NZ, NYL, NC, NYH, NX = 16, 2, 2, 2, 4


def unit(v, axis):
    v = v.astype(F32)
    norms = jnp.sqrt(jnp.sum(v * v, axis=axis, keepdims=True) + 1e-06)
    return v / norms, norms


def gather_t(v):
    return lax.all_gather(lax.all_gather(v, "yh", axis=0, tiled=True), "x", axis=0, tiled=True)


def split_float(v):
    high = lax.reduce_precision(v, 8, 7)
    return high.astype(BF), (v - high).astype(BF)


def per_device(pooled, texts, head_w, log_scale, bias):
    z, yl, c = lax.axis_index("z"), lax.axis_index("yl"), lax.axis_index("c")
    yh, x = lax.axis_index("yh"), lax.axis_index("x")
    rows, width = pooled.shape
    cols = head_w.shape[0]
    scale = jnp.exp(log_scale[0])
    shift = bias[0]

    text_unit = unit(texts, 1)[0].astype(BF)
    text_pair = lax.all_gather(text_unit, "yl", axis=0, tiled=True)
    text_own = lax.all_gather(text_pair, "z", axis=0, tiled=True)
    text_other = lax.ppermute(text_own, "c", [(0, 1), (1, 0)])

    images = gather_t(pooled)
    count = images.shape[0]
    own_cols = lax.dot_general(
        head_w, images, (((1,), (1,)), ((), ())), preferred_element_type=F32
    ).astype(BF)
    proj = gather_t(own_cols).reshape(NX, NYH, cols, count)
    proj = proj.transpose(1, 0, 2, 3).reshape(width, count)
    unit_all, norms = unit(proj, 0)
    embedded = unit_all.astype(BF)

    small = width // (NZ * NYL * NC)
    padded = -(-small // 16) * 16
    parts = images.T.reshape(NZ, NYL * NC, small, count).transpose(1, 0, 2, 3)
    parts = jnp.pad(parts, ((0, 0), (0, 0), (0, padded - small), (0, 0)))
    parts = lax.all_to_all(parts, ("yl", "c"), split_axis=0, concat_axis=0, tiled=True)

    def half(text, masked):
        scores = jnp.dot(text, embedded, preferred_element_type=F32)
        logits = scale * scores + shift
        if masked:
            a = lax.broadcasted_iota(jnp.int32, logits.shape, 0) - (z * NYL + yl) * rows
            b = lax.broadcasted_iota(jnp.int32, logits.shape, 1) - (x * NYH + yh) * rows
            sign = jnp.where((a == b) & (a >= 0) & (a < rows), -1.0, 1.0).astype(F32)
            pair = (sign * jax.nn.sigmoid(sign * logits)).astype(BF)
        else:
            pair = jax.nn.sigmoid(logits).astype(BF)
        terms = lax.dot_general(
            text, pair, (((0,), (0,)), ((), ())), preferred_element_type=F32
        )
        return terms, jnp.sum(pair.astype(F32) * scores, axis=0)

    terms_own, dots_own = half(text_own, True)
    terms_other, dots_other = half(text_other, False)
    terms = (terms_own + terms_other).astype(BF).reshape(NYH * NX, cols, count)
    high, low = split_float(dots_own + dots_other)
    dots = jnp.stack([high, low] + [jnp.zeros_like(high)] * 14)
    block = jnp.concatenate([terms, jnp.broadcast_to(dots, (NYH * NX, 16, count))], axis=1)
    block = lax.all_to_all(block, T, split_axis=0, concat_axis=0, tiled=True)
    block = scale * jnp.sum(block.astype(F32), axis=0)
    row_dots = block[cols : cols + 1] + block[cols + 1 : cols + 2]
    own_unit = own_cols.astype(F32) / norms
    grad_proj = ((block[:cols] - own_unit * row_dots) / norms).astype(BF)

    grad_pooled = lax.dot_general(
        grad_proj, head_w, (((0,), (0,)), ((), ())), preferred_element_type=F32
    ).astype(BF)
    grad_pooled = lax.psum_scatter(grad_pooled, "x", scatter_dimension=0, tiled=True)
    grad_pooled = lax.psum_scatter(grad_pooled, "yh", scatter_dimension=0, tiled=True)

    grad_all = lax.all_gather(grad_proj, ("yl", "c"), axis=0)
    grad_head = jnp.einsum("szri,sfi->zrf", parts, grad_all, preferred_element_type=F32).astype(BF)
    grad_head = lax.all_to_all(grad_head, "z", split_axis=0, concat_axis=0, tiled=True)
    grad_head = jnp.sum(grad_head.astype(F32), axis=0)[:small]
    return (grad_pooled.astype(F32), grad_head)


def solution(mesh):
    fine = Mesh(mesh.devices.reshape(NZ, NYL, NC, NYH, NX), ("z", "yl", "c", "yh", "x"))
    dp = ("z", "yl", "c")
    rows = P(dp + T, None)
    return jax.shard_map(
        per_device,
        mesh=fine,
        in_specs=(rows, rows, P(T, None), P(), P()),
        out_specs=(rows, P(dp, T)),
        check_vma=False,
    )
```

time: 782 us -> 247 us (0.32)
  waiting for transfers between devices: 666 us -> 107 us
  starting transfers between devices: 0.16 us -> 14.1 us
  blocking collectives: 72.7 us -> 81.7 us
    unnamed x5 -> x3, waiting for transfers between devices: 419 us -> 0.69 us
    psum x1 -> x0, waiting for transfers between devices: 97.1 us -> none  [per_device(): lax.psum(text_terms.astype(jnp.bfloat16), 'tensor').astype(jnp.float32)]
    reduce_scatter x1 -> x2, waiting for transfers between devices: 92 us -> 6.1 us  [the longest x1 6.08 us: per_device(): lax.psum_scatter(grad_pooled, 'yh', scatter_dimension=0, tiled=True)]
    all_gather x1, waiting for transfers between devices: 58.1 us -> 81.8 us  [per_device(): text_own = lax.all_gather(text_pair, 'z', axis=0, tiled=True)]
    all_to_all x0 -> x2, waiting for transfers between devices: none -> 18 us  [the longest x1 18 us: per_device(): lax.all_to_all(grad_head, 'z', split_axis=0, concat_axis=0, tiled=True)]
    all_to_all x0 -> x1, blocking collectives: none -> 17.2 us  [per_device(): block = lax.all_to_all(block, T, split_axis=0, concat_axis=0, tiled=True)]
    all_to_all x0 -> x2, starting transfers between devices: none -> 12.1 us  [the longest x1 7.89 us: per_device(): lax.all_to_all(grad_head, 'z', split_axis=0, concat_axis=0, tiled=True)]
    all_gather x2 -> x6, blocking collectives: 72.7 us -> 64.4 us  [the longest x2 27.7 us: gather_t(): lax.all_gather(lax.all_gather(v, 'yh', axis=0, tiled=True), 'x', axis=0,...]
  transfers between devices with their start and end apart: 4 -> 6, of which waited for: 4 -> 3; matrix products, arithmetic and copies ran while one was open for 1% -> 5% of each run, Pallas kernels for 0% -> 0%
where the time goes in v1:
time: 247 us; the launch traced here: 244 us
  waiting for transfers between devices  107 us (43%)
  blocking collectives  81.7 us (33%)
  matrix products  15.8 us (6%)
  between operations  15.6 us (6%)
  starting transfers between devices  14.1 us (6%)
  other arithmetic  6.61 us (3%)
  local copies, waits for them, and re-layouts  3.44 us (1%)
    all_gather x1, waiting for transfers between devices, per_device(): text_own = lax.all_gather(text_pair, 'z', axis=0, tiled=True)  81.8 us
    all_gather x2, blocking collectives, gather_t(): lax.all_gather(lax.all_gather(v, 'yh', axis=0, tiled=True), 'x', axis=0,...  27.7 us
    all_to_all x1, waiting for transfers between devices, per_device(): lax.all_to_all(grad_head, 'z', split_axis=0, concat_axis=0, tiled=True)  18 us
    all_to_all x1, blocking collectives, per_device(): block = lax.all_to_all(block, T, split_axis=0, concat_axis=0, tiled=True)  17.2 us
    all_gather x1, blocking collectives, per_device(): grad_all = lax.all_gather(grad_proj, ('yl', 'c'), axis=0)  16.1 us
    all_gather x2, blocking collectives, gather_t(): lax.all_gather(v, 'yh', axis=0, tiled=True)  14.9 us
    all_to_all x1, starting transfers between devices, per_device(): lax.all_to_all(grad_head, 'z', split_axis=0, concat_axis=0, tiled=True)  7.89 us
    dot_general x2, matrix products, half(): lax.dot_general(text, pair, (((0,), (0,)), ((), ())), preferred_element_t...  7.23 us
  transfers between devices with their start and end apart: 6, of which 3 were waited for; matrix products, arithmetic and copies ran while one was open for 5% of the time, Pallas kernels for 0%

profile of v1, /device:TPU:24, one launch (start us, length us, event | category | flops | bytes accessed | tf_op | source)
XLA Modules:
  0.0 243.8 jit_solution(7370888235062188037)
XLA Ops:
  7.2 1.1 fusion.8
  8.3 1.0 fusion.9
  9.3 5.7 %all_gather.24 = bf16[64,1792]{1,0:T(8,128)(2,1)} all-gather(bf16[32,1792]{1,0:T(8,128)(2,1)S(1)} %fusion.9), channel_id=1, replica_groups=mesh['z'=16,'yl'=2,'c'=2,'yh'=2,'x'=4] {'yl'}, dimensions={0}, use_global_device_ids=true | all-gather | bytes 344064 | tf_op jit(solution)/shard_map/all_gather | solution.py:36
  15.1 81.8 %all-gather.3.cloned.1.call-done = bf16[1024,1792]{1,0:T(8,128)(2,1)} async-done(((bf16[64,1792]{1,0:T(8,128)(2,1)}), bf16[1024,1792]{1,0:T(8,128)(2,1)}) %all-gather.3.cloned.1.call-update) | async-done | bytes 3670032 | tf_op jit(solution)/shard_map/all_gather | solution.py:37
  96.8 1.9 collective-permute-start
  98.8 7.9 %all_gather.26 = bf16[64,1792]{1,0:T(8,128)(2,1)S(1)} all-gather(bf16[32,1792]{1,0:T(8,128)(2,1)} %param.5), channel_id=1, replica_groups=mesh['z'=16,'yl'=2,'c'=2,'yh'=2,'x'=4] {'yh'}, dimensions={0}, use_global_device_ids=true | all-gather | bytes 344064 | tf_op jit(solution)/shard_map/all_gather | solution.py:19
  106.7 13.9 %all_gather.27 = bf16[256,1792]{1,0:T(8,128)(2,1)S(1)} all-gather(bf16[64,1792]{1,0:T(8,128)(2,1)S(1)} %all_gather.26), channel_id=1, replica_groups=mesh['z'=16,'yl'=2,'c'=2,'yh'=2,'x'=4] {'x'}, dimensions={0}, use_global_device_ids=true | all-gather | bytes 1146880 | tf_op jit(solution)/shard_map/all_gather | solution.py:19
  120.6 0.5 convolution_convert_fusion.1
  121.0 7.0 %all_gather.28 = bf16[448,256]{1,0:T(8,128)(2,1)S(1)} all-gather(bf16[224,256]{1,0:T(8,128)(2,1)S(1)} %convolution_convert_fusion.1), channel_id=1, replica_groups=mesh['z'=16,'yl'=2,'c'=2,'yh'=2,'x'=4] {'yh'}, dimensions={0}, use_global_device_ids=true | all-gather | bytes 344064 | tf_op jit(solution)/shard_map/all_gather | solution.py:19
  128.0 13.8 %all_gather.29 = bf16[1792,256]{1,0:T(8,128)(2,1)S(1)} all-gather(bf16[448,256]{1,0:T(8,128)(2,1)S(1)} %all_gather.28), channel_id=1, replica_groups=mesh['z'=16,'yl'=2,'c'=2,'yh'=2,'x'=4] {'x'}, dimensions={0}, use_global_device_ids=true | all-gather | bytes 1146880 | tf_op jit(solution)/shard_map/all_gather | solution.py:19
  141.8 1.5 copy.10
  145.1 0.3 multiply_reduce_fusion
  145.3 1.6 fusion.1
  147.0 1.4 multiply_reduce_fusion.2
  148.4 3.0 %fusion.15 = f32[1792,256]{1,0:T(8,128)} fusion(bf16[1024,1792]{1,0:T(8,128)(2,1)S(1)} %copy-done.1, f32[1024,256]{1,0:T(8,128)S(1)} %get-tuple-element.5, f32[]{:T(128)} %bitcast.37, f32[]{:T(128)} %bitcast, s32[256]{0:T(256)S(1)} %iota_subtract_fusion.1, s32[1024]{0:T(1024)S(1)} %iota_subtract_fusion, pred[1024]{0:T(1024)(128)(4,1)S(1)} %get-tuple-element.8, ...), kind=kOutput, calls=%fused_computation.40 | convolution fusion | flops 942669824 | bytes 6560776 | tf_op jit(solution)/shard_map/dot_general | solution.py:66
  151.4 4.2 %multiply_reduce_fusion.1 = (f32[256]{0:T(256)S(1)}, f32[1024,256]{1,0:T(8,128)}) fusion(f32[]{:T(128)} %bitcast.39, f32[]{:T(128)} %bitcast, bf16[1024,1792]{1,0:T(8,128)(2,1)} %collective-permute-done, bf16[1792,256]{1,0:T(8,128)(2,1)S(1)} %fusion.1), kind=kOutput, calls=%fused_computation.16 | convolution fusion | flops 941883136 | bytes 5637128 | tf_op jit(solution)/shard_map/dot_general | solution.py:57
  155.7 4.2 %fusion = bf16[1792,256]{1,0:T(8,128)(2,1)S(1)} fusion(f32[1792,256]{1,0:T(8,128)} %fusion.15, bf16[1024,1792]{1,0:T(8,128)(2,1)} %collective-permute-done, f32[1024,256]{1,0:T(8,128)} %get-tuple-element.7, f32[]{:T(128)} %bitcast.38, f32[]{:T(128)} %bitcast), kind=kOutput, calls=%fused_computation.2 | convolution fusion | flops 942014464 | bytes 7471112 | tf_op jit(solution)/shard_map/dot_general | solution.py:66
  160.0 17.2 %all_to_all.15 = bf16[8,240,256]{2,1,0:T(8,128)(2,1)S(1)} all-to-all(bf16[8,240,256]{2,1,0:T(8,128)(2,1)S(1)} %pad_maximum_fusion), channel_id=1, replica_groups=mesh['z'=16,'yl'=2,'c'=2,'yh'=2,'x'=4] {'yh','x'}, dimensions={0} | all-to-all | bytes 1966080 | tf_op jit(solution)/shard_map/all_to_all | solution.py:77
  177.2 0.1 convert_reduce_fusion
  177.5 1.4 convolution_convert_fusion
  178.9 0.5 copy.11
  179.4 0.2 reshape.64
  179.7 1.1 pad.4.clone
  180.8 4.2 %all-to-all-start.1 = ((bf16[4,16,32,256]{3,2,1,0:T(8,128)(2,1)}), bf16[4,16,32,256]{3,2,1,0:T(8,128)(2,1)S(1)}, u32[]{:S(2)}, u32[]{:S(2)}) async-start(bf16[4,16,32,256]{3,2,1,0:T(8,128)(2,1)} %pad.4.clone), calls=%async_computation.3 | async-start | bytes 2097152 | tf_op jit(solution)/shard_map/all_to_all | solution.py:54
  185.0 16.1 %all-gather = bf16[896,256]{1,0:T(8,128)(2,1)S(1)} all-gather(bf16[224,256]{1,0:T(8,128)(2,1)S(1)} %fusion.11), channel_id=2, replica_groups=mesh['z'=16,'yl'=2,'c'=2,'yh'=2,'x'=4] {'yl','c'}, dimensions={0}, use_global_device_ids=true | all-gather | bytes 573440 | tf_op jit(solution)/shard_map/all_gather | solution.py:89
  201.1 1.2 fusion.2
  202.3 7.9 %all-to-all-start.2 = ((bf16[16,32,224]{2,1,0:T(8,128)(2,1)}), bf16[16,32,224]{2,1,0:T(8,128)(2,1)S(1)}, u32[]{:S(2)}, u32[]{:S(2)}) async-start(bf16[16,32,224]{2,1,0:T(8,128)(2,1)} %fusion.2), calls=%async_computation.4 | async-start | bytes 524288 | tf_op jit(solution)/shard_map/all_to_all | solution.py:91
  210.2 0.7 reduce-scatter.5.cloned.1.call-update
  210.9 18.0 %all-to-all-done.2 = bf16[16,32,224]{2,1,0:T(8,128)(2,1)S(1)} async-done(((bf16[16,32,224]{2,1,0:T(8,128)(2,1)}), bf16[16,32,224]{2,1,0:T(8,128)(2,1)S(1)}, u32[]{:S(2)}, u32[]{:S(2)}) %all-to-all-start.2) | async-done | bytes 229408 | tf_op jit(solution)/shard_map/all_to_all | solution.py:91
  228.9 0.7 convert_reduce_fusion.1
  229.5 6.1 %reduce-scatter.5.cloned.1.call-done = bf16[32,1792]{1,0:T(8,128)(2,1)} async-done(((bf16[64,1792]{1,0:T(8,128)(2,1)}), bf16[32,1792]{1,0:T(8,128)(2,1)}) %reduce-scatter.5.cloned.1.call-update) | async-done | bytes 114704 | tf_op jit(solution)/shard_map/reduce_scatter | solution.py:87
  235.6 1.6 convert_element_type.107
  (29 shorter events, 0.5 us)
Async XLA Ops:
  7.2 113.4 %copy-start = (bf16[224,1792]{1,0:T(8,128)(2,1)S(1)}, bf16[224,1792]{1,0:T(8,128)(2,1)}, u32[]{:S(2)}) copy-start(bf16[224,1792]{1,0:T(8,128)(2,1)} %param.7) | copy-start | bytes 2408452
  7.2 89.7 %all-gather.3.cloned.1.call-start = ((), (), s32[]{:S(2)}) async-start(), calls=%async_computation.5 | async-start | bytes 3899392 | tf_op jit(solution)/shard_map/all_gather | solution.py:37
  15.0 195.2 %reduce-scatter.3.cloned.1.call-start = ((), (), s32[]{:S(2)}) async-start(), calls=%async_computation.6 | async-start | bytes 1146880 | tf_op jit(solution)/shard_map/reduce_scatter | solution.py:86
  96.8 54.6 %collective-permute-start = (bf16[1024,1792]{1,0:T(8,128)(2,1)}, bf16[1024,1792]{1,0:T(8,128)(2,1)}, u32[]{:S(2)}, u32[]{:S(2)}) collective-permute-start(bf16[1024,1792]{1,0:T(8,128)(2,1)} %all-gather.3.cloned.1.call-done), channel_id=1, source_target_pairs={{0,8},{8,0},{1,9},{9,1},{2,10},{10,2},{3,11},{11,3},{4,12},{12,4},... | collective-permute-start | bytes 11010056 | tf_op jit(solution)/shard_map/ppermute | solution.py:38
  143.3 3.7 %copy-start.1 = (bf16[1024,1792]{1,0:T(8,128)(2,1)S(1)}, bf16[1024,1792]{1,0:T(8,128)(2,1)}, u32[]{:S(2)}) copy-start(bf16[1024,1792]{1,0:T(8,128)(2,1)} %all-gather.3.cloned.1.call-done) | copy-start | bytes 11010052
  180.8 20.3 %all-to-all-start.1 = ((bf16[4,16,32,256]{3,2,1,0:T(8,128)(2,1)}), bf16[4,16,32,256]{3,2,1,0:T(8,128)(2,1)S(1)}, u32[]{:S(2)}, u32[]{:S(2)}) async-start(bf16[4,16,32,256]{3,2,1,0:T(8,128)(2,1)} %pad.4.clone), calls=%async_computation.3 | async-start | bytes 2097152 | tf_op jit(solution)/shard_map/all_to_all | solution.py:54
  202.3 26.6 %all-to-all-start.2 = ((bf16[16,32,224]{2,1,0:T(8,128)(2,1)}), bf16[16,32,224]{2,1,0:T(8,128)(2,1)S(1)}, u32[]{:S(2)}, u32[]{:S(2)}) async-start(bf16[16,32,224]{2,1,0:T(8,128)(2,1)} %fusion.2), calls=%async_computation.4 | async-start | bytes 524288 | tf_op jit(solution)/shard_map/all_to_all | solution.py:91
  210.1 25.5 %reduce-scatter.5.cloned.1.call-start = ((), (), s32[]{:S(2)}) async-start(), calls=%async_computation.7 | async-start | bytes 344064 | tf_op jit(solution)/shard_map/reduce_scatter | solution.py:87
Sparse Core Ops, SparseCore 0:
  15.1 81.6 all-gather.2
  179.0 25.9 reduce-scatter.2
  213.8 21.8 reduce-scatter.4

commit v2 on v1

--- a/solution.py
+++ b/solution.py
@@ -35,7 +35,6 @@
     text_unit = unit(texts, 1)[0].astype(BF)
     text_pair = lax.all_gather(text_unit, "yl", axis=0, tiled=True)
     text_own = lax.all_gather(text_pair, "z", axis=0, tiled=True)
-    text_other = lax.ppermute(text_own, "c", [(0, 1), (1, 0)])
 
     images = gather_t(pooled)
     count = images.shape[0]
@@ -52,6 +51,11 @@
     parts = images.T.reshape(NZ, NYL * NC, small, count).transpose(1, 0, 2, 3)
     parts = jnp.pad(parts, ((0, 0), (0, 0), (0, padded - small), (0, 0)))
     parts = lax.all_to_all(parts, ("yl", "c"), split_axis=0, concat_axis=0, tiled=True)
+
+    text_own, embedded, norms, parts = lax.optimization_barrier(
+        (text_own, embedded, norms, parts)
+    )
+    text_other = lax.ppermute(text_own, "c", [(0, 1), (1, 0)])
 
     def half(text, masked):
         scores = jnp.dot(text, embedded, preferred_element_type=F32)

time: 247 us -> 200 us (0.81)
  waiting for transfers between devices: 107 us -> 49.9 us
  blocking collectives: 81.7 us -> 88.6 us
    all_gather x1, waiting for transfers between devices: 81.8 us -> 15.7 us  [per_device(): text_own = lax.all_gather(text_pair, 'z', axis=0, tiled=True)]
    all_gather x2, blocking collectives: 14.9 us -> 26.9 us  [gather_t(): lax.all_gather(v, 'yh', axis=0, tiled=True)]
    reduce_scatter x1, waiting for transfers between devices: 0.02 us -> 10.8 us  [per_device(): lax.psum_scatter(grad_pooled, 'x', scatter_dimension=0, tiled=True)]
    all_to_all x1, waiting for transfers between devices: 18 us -> 7.89 us  [per_device(): lax.all_to_all(grad_head, 'z', split_axis=0, concat_axis=0, tiled=True)]
    all_gather x1, blocking collectives: 16.1 us -> 6.33 us  [per_device(): grad_all = lax.all_gather(grad_proj, ('yl', 'c'), axis=0)]
    reduce_scatter x1, waiting for transfers between devices: 6.08 us -> 15.5 us  [per_device(): lax.psum_scatter(grad_pooled, 'yh', scatter_dimension=0, tiled=True)]
    all_to_all x1, blocking collectives: 17.2 us -> 21.1 us  [per_device(): block = lax.all_to_all(block, T, split_axis=0, concat_axis=0, tiled=True)]
  transfers between devices with their start and end apart: 6 -> 6, of which waited for: 3 -> 4; matrix products, arithmetic and copies ran while one was open for 5% -> 7% of each run, Pallas kernels for 0% -> 0%
where the time goes in v2:
time: 200 us; the launch traced here: 196 us
  blocking collectives  88.6 us (44%)
  waiting for transfers between devices  49.9 us (25%)
  matrix products  17.8 us (9%)
  starting transfers between devices  15.9 us (8%)
  between operations  15.3 us (8%)
  other arithmetic  5.11 us (3%)
  local copies, waits for them, and re-layouts  3.92 us (2%)
    all_gather x2, blocking collectives, gather_t(): lax.all_gather(lax.all_gather(v, 'yh', axis=0, tiled=True), 'x', axis=0,...  28.6 us
    all_gather x2, blocking collectives, gather_t(): lax.all_gather(v, 'yh', axis=0, tiled=True)  26.9 us
    all_to_all x1, blocking collectives, per_device(): block = lax.all_to_all(block, T, split_axis=0, concat_axis=0, tiled=True)  21.1 us
    all_gather x1, waiting for transfers between devices, per_device(): text_own = lax.all_gather(text_pair, 'z', axis=0, tiled=True)  15.7 us
    reduce_scatter x1, waiting for transfers between devices, per_device(): lax.psum_scatter(grad_pooled, 'yh', scatter_dimension=0, tiled=True)  15.5 us
    reduce_scatter x1, waiting for transfers between devices, per_device(): lax.psum_scatter(grad_pooled, 'x', scatter_dimension=0, tiled=True)  10.8 us
    all_to_all x1, starting transfers between devices, per_device(): lax.all_to_all(grad_head, 'z', split_axis=0, concat_axis=0, tiled=True)  7.91 us
    all_to_all x1, waiting for transfers between devices, per_device(): lax.all_to_all(grad_head, 'z', split_axis=0, concat_axis=0, tiled=True)  7.89 us
  transfers between devices with their start and end apart: 6, of which 4 were waited for; matrix products, arithmetic and copies ran while one was open for 7% of the time, Pallas kernels for 0%

profile of v2, /device:TPU:24, one launch (start us, length us, event | category | flops | bytes accessed | tf_op | source)
XLA Modules:
  0.0 196.4 jit_solution(9552093433629099625)
XLA Ops:
  7.2 1.1 fusion.8
  8.3 1.0 fusion.9
  9.3 5.7 %all_gather.24 = bf16[64,1792]{1,0:T(8,128)(2,1)} all-gather(bf16[32,1792]{1,0:T(8,128)(2,1)S(1)} %fusion.9), channel_id=1, replica_groups=mesh['z'=16,'yl'=2,'c'=2,'yh'=2,'x'=4] {'yl'}, dimensions={0}, use_global_device_ids=true | all-gather | bytes 344064 | tf_op jit(solution)/shard_map/all_gather | solution.py:36
  15.0 9.0 %all_gather.26 = bf16[64,1792]{1,0:T(8,128)(2,1)S(1)} all-gather(bf16[32,1792]{1,0:T(8,128)(2,1)} %param.5), channel_id=1, replica_groups=mesh['z'=16,'yl'=2,'c'=2,'yh'=2,'x'=4] {'yh'}, dimensions={0}, use_global_device_ids=true | all-gather | bytes 344064 | tf_op jit(solution)/shard_map/all_gather | solution.py:19
  24.0 13.7 %all_gather.27 = bf16[256,1792]{1,0:T(8,128)(2,1)S(1)} all-gather(bf16[64,1792]{1,0:T(8,128)(2,1)S(1)} %all_gather.26), channel_id=1, replica_groups=mesh['z'=16,'yl'=2,'c'=2,'yh'=2,'x'=4] {'x'}, dimensions={0}, use_global_device_ids=true | all-gather | bytes 1146880 | tf_op jit(solution)/shard_map/all_gather | solution.py:19
  37.8 1.3 copy.11
  39.1 1.3 reshape.72
  40.4 1.1 pad.4.clone
  41.5 6.0 %all-to-all-start = ((bf16[4,16,32,256]{3,2,1,0:T(8,128)(2,1)}), bf16[4,16,32,256]{3,2,1,0:T(8,128)(2,1)S(1)}, u32[]{:S(2)}, u32[]{:S(2)}) async-start(bf16[4,16,32,256]{3,2,1,0:T(8,128)(2,1)} %pad.4.clone), calls=%async_computation | async-start | bytes 2097152 | tf_op jit(solution)/shard_map/all_to_all | solution.py:53
  47.5 0.5 convolution_convert_fusion.1
  47.9 17.9 %all_gather.28 = bf16[448,256]{1,0:T(8,128)(2,1)S(1)} all-gather(bf16[224,256]{1,0:T(8,128)(2,1)S(1)} %convolution_convert_fusion.1), channel_id=1, replica_groups=mesh['z'=16,'yl'=2,'c'=2,'yh'=2,'x'=4] {'yh'}, dimensions={0}, use_global_device_ids=true | all-gather | bytes 344064 | tf_op jit(solution)/shard_map/all_gather | solution.py:19
  65.8 14.8 %all_gather.29 = bf16[1792,256]{1,0:T(8,128)(2,1)S(1)} all-gather(bf16[448,256]{1,0:T(8,128)(2,1)S(1)} %all_gather.28), channel_id=1, replica_groups=mesh['z'=16,'yl'=2,'c'=2,'yh'=2,'x'=4] {'x'}, dimensions={0}, use_global_device_ids=true | all-gather | bytes 1146880 | tf_op jit(solution)/shard_map/all_gather | solution.py:19
  80.6 0.3 multiply_reduce_fusion
  80.9 0.2 copy.10
  81.1 0.2 fusion.1
  81.3 15.7 %all-gather.3.cloned.1.call-done = bf16[1024,1792]{1,0:T(8,128)(2,1)} async-done(((bf16[64,1792]{1,0:T(8,128)(2,1)}), bf16[1024,1792]{1,0:T(8,128)(2,1)}) %all-gather.3.cloned.1.call-update) | async-done | bytes 3670032 | tf_op jit(solution)/shard_map/all_gather | solution.py:37
  96.9 1.9 collective-permute-start
  100.2 3.4 %multiply_reduce_fusion.2 = (f32[256]{0:T(256)S(1)}, f32[1024,256]{1,0:T(8,128)S(1)}) fusion(f32[]{:T(128)} %bitcast.42, f32[]{:T(128)} %bitcast, pred[1024]{0:T(1024)(128)(4,1)S(1)} %get-tuple-element.16, pred[1024]{0:T(1024)(128)(4,1)S(1)} %get-tuple-element.17, s32[256]{0:T(256)S(1)} %iota_subtract_fusion.1, s32[1024]{0:T(1024)S(1)} %iota_subtract_fusion, ...), kind=kOutput, calls=%fused_computation.17 | convolution fusion | flops 943456000 | bytes 5644296 | tf_op jit(solution)/shard_map/dot_general | solution.py:61
  103.6 3.1 %fusion.15 = f32[1792,256]{1,0:T(8,128)} fusion(bf16[1024,1792]{1,0:T(8,128)(2,1)S(1)} %copy-done.1, f32[1024,256]{1,0:T(8,128)S(1)} %get-tuple-element.13, f32[]{:T(128)} %bitcast.39, f32[]{:T(128)} %bitcast, s32[256]{0:T(256)S(1)} %iota_subtract_fusion.1, s32[1024]{0:T(1024)S(1)} %iota_subtract_fusion, pred[1024]{0:T(1024)(128)(4,1)S(1)} %get-tuple-element.16, ...), kind=kOutput, calls=%fused_computation.40 | convolution fusion | flops 942669824 | bytes 6560776 | tf_op jit(solution)/shard_map/dot_general | solution.py:70
  106.7 4.2 %multiply_reduce_fusion.1 = (f32[256]{0:T(256)S(1)}, f32[1024,256]{1,0:T(8,128)}) fusion(f32[]{:T(128)} %bitcast.41, f32[]{:T(128)} %bitcast, bf16[1024,1792]{1,0:T(8,128)(2,1)} %collective-permute-done, bf16[1792,256]{1,0:T(8,128)(2,1)S(1)} %fusion.1), kind=kOutput, calls=%fused_computation.16 | convolution fusion | flops 941883136 | bytes 5637128 | tf_op jit(solution)/shard_map/dot_general | solution.py:61
  110.9 4.2 %fusion = bf16[1792,256]{1,0:T(8,128)(2,1)S(1)} fusion(f32[1792,256]{1,0:T(8,128)} %fusion.15, bf16[1024,1792]{1,0:T(8,128)(2,1)} %collective-permute-done, f32[1024,256]{1,0:T(8,128)} %get-tuple-element.15, f32[]{:T(128)} %bitcast.40, f32[]{:T(128)} %bitcast), kind=kOutput, calls=%fused_computation.2 | convolution fusion | flops 942014464 | bytes 7471112 | tf_op jit(solution)/shard_map/dot_general | solution.py:70
  115.2 21.1 %all_to_all.15 = bf16[8,240,256]{2,1,0:T(8,128)(2,1)S(1)} all-to-all(bf16[8,240,256]{2,1,0:T(8,128)(2,1)S(1)} %pad_maximum_fusion), channel_id=1, replica_groups=mesh['z'=16,'yl'=2,'c'=2,'yh'=2,'x'=4] {'yh','x'}, dimensions={0} | all-to-all | bytes 1966080 | tf_op jit(solution)/shard_map/all_to_all | solution.py:81
  136.3 0.1 convert_reduce_fusion
  136.6 1.4 convolution_convert_fusion
  138.0 6.3 %all-gather = bf16[896,256]{1,0:T(8,128)(2,1)S(1)} all-gather(bf16[224,256]{1,0:T(8,128)(2,1)S(1)} %fusion.11), channel_id=2, replica_groups=mesh['z'=16,'yl'=2,'c'=2,'yh'=2,'x'=4] {'yl','c'}, dimensions={0}, use_global_device_ids=true | all-gather | bytes 573440 | tf_op jit(solution)/shard_map/all_gather | solution.py:93
  144.3 1.2 fusion.2
  145.5 7.9 %all-to-all-start.2 = ((bf16[16,32,224]{2,1,0:T(8,128)(2,1)}), bf16[16,32,224]{2,1,0:T(8,128)(2,1)S(1)}, u32[]{:S(2)}, u32[]{:S(2)}) async-start(bf16[16,32,224]{2,1,0:T(8,128)(2,1)} %fusion.2), calls=%async_computation.4 | async-start | bytes 524288 | tf_op jit(solution)/shard_map/all_to_all | solution.py:95
  153.4 10.8 %reduce-scatter.3.cloned.1.call-done = bf16[64,1792]{1,0:T(8,128)(2,1)} async-done(((bf16[256,1792]{1,0:T(8,128)(2,1)}), bf16[64,1792]{1,0:T(8,128)(2,1)}) %reduce-scatter.3.cloned.1.call-update) | async-done | bytes 229392 | tf_op jit(solution)/shard_map/reduce_scatter | solution.py:90
  164.2 7.9 %all-to-all-done.2 = bf16[16,32,224]{2,1,0:T(8,128)(2,1)S(1)} async-done(((bf16[16,32,224]{2,1,0:T(8,128)(2,1)}), bf16[16,32,224]{2,1,0:T(8,128)(2,1)S(1)}, u32[]{:S(2)}, u32[]{:S(2)}) %all-to-all-start.2) | async-done | bytes 229408 | tf_op jit(solution)/shard_map/all_to_all | solution.py:95
  172.1 0.7 convert_reduce_fusion.1
  172.8 15.5 %reduce-scatter.5.cloned.1.call-done = bf16[32,1792]{1,0:T(8,128)(2,1)} async-done(((bf16[64,1792]{1,0:T(8,128)(2,1)}), bf16[32,1792]{1,0:T(8,128)(2,1)}) %reduce-scatter.5.cloned.1.call-update) | async-done | bytes 114704 | tf_op jit(solution)/shard_map/reduce_scatter | solution.py:91
  188.3 1.6 convert_element_type.107
  (29 shorter events, 0.5 us)
Async XLA Ops:
  7.2 40.3 %copy-start = (bf16[224,1792]{1,0:T(8,128)(2,1)S(1)}, bf16[224,1792]{1,0:T(8,128)(2,1)}, u32[]{:S(2)}) copy-start(bf16[224,1792]{1,0:T(8,128)(2,1)} %param.7) | copy-start | bytes 2408452
  7.2 89.8 %all-gather.3.cloned.1.call-start = ((), (), s32[]{:S(2)}) async-start(), calls=%async_computation.5 | async-start | bytes 3899392 | tf_op jit(solution)/shard_map/all_gather | solution.py:37
  41.5 39.7 %all-to-all-start = ((bf16[4,16,32,256]{3,2,1,0:T(8,128)(2,1)}), bf16[4,16,32,256]{3,2,1,0:T(8,128)(2,1)S(1)}, u32[]{:S(2)}, u32[]{:S(2)}) async-start(bf16[4,16,32,256]{3,2,1,0:T(8,128)(2,1)} %pad.4.clone), calls=%async_computation | async-start | bytes 2097152 | tf_op jit(solution)/shard_map/all_to_all | solution.py:53
  47.5 116.7 %reduce-scatter.3.cloned.1.call-start = ((), (), s32[]{:S(2)}) async-start(), calls=%async_computation.6 | async-start | bytes 1146880 | tf_op jit(solution)/shard_map/reduce_scatter | solution.py:90
  96.9 9.7 %collective-permute-start = (bf16[1024,1792]{1,0:T(8,128)(2,1)}, bf16[1024,1792]{1,0:T(8,128)(2,1)}, u32[]{:S(2)}, u32[]{:S(2)}) collective-permute-start(bf16[1024,1792]{1,0:T(8,128)(2,1)} %all-gather.3.cloned.1.call-done), channel_id=1, source_target_pairs={{0,8},{8,0},{1,9},{9,1},{2,10},{10,2},{3,11},{11,3},{4,12},{12,4},... | collective-permute-start | bytes 11010056 | tf_op jit(solution)/shard_map/ppermute | solution.py:58
  100.2 3.4 %copy-start.1 = (bf16[1024,1792]{1,0:T(8,128)(2,1)S(1)}, bf16[1024,1792]{1,0:T(8,128)(2,1)}, u32[]{:S(2)}) copy-start(bf16[1024,1792]{1,0:T(8,128)(2,1)} %all-gather.3.cloned.1.call-done) | copy-start | bytes 11010052
  145.5 26.6 %all-to-all-start.2 = ((bf16[16,32,224]{2,1,0:T(8,128)(2,1)}), bf16[16,32,224]{2,1,0:T(8,128)(2,1)S(1)}, u32[]{:S(2)}, u32[]{:S(2)}) async-start(bf16[16,32,224]{2,1,0:T(8,128)(2,1)} %fusion.2), calls=%async_computation.4 | async-start | bytes 524288 | tf_op jit(solution)/shard_map/all_to_all | solution.py:95
  153.4 34.9 %reduce-scatter.5.cloned.1.call-start = ((), (), s32[]{:S(2)}) async-start(), calls=%async_computation.7 | async-start | bytes 344064 | tf_op jit(solution)/shard_map/reduce_scatter | solution.py:91
Sparse Core Ops, SparseCore 0:
  15.1 81.7 all-gather.2
  138.1 26.0 reduce-scatter.2
  167.0 21.2 reduce-scatter.4

commit v3 on v1

v3 whole, which is shorter than its diff:
```python
import jax
import jax.numpy as jnp
from jax import lax
from jax.experimental import pallas as pl
from jax.experimental.pallas import tpu as pltpu
from jax.sharding import Mesh, PartitionSpec as P

BF = jnp.bfloat16
F32 = jnp.float32
T = ("yh", "x")
NZ, NYL, NC, NYH, NX = 16, 2, 2, 2, 4
CORES = [(0, 1), (1, 0)]


def unit(v, axis):
    v = v.astype(F32)
    norms = jnp.sqrt(jnp.sum(v * v, axis=axis, keepdims=True) + 1e-06)
    return v / norms, norms


def gather_t(v):
    return lax.all_gather(lax.all_gather(v, "yh", axis=0, tiled=True), "x", axis=0, tiled=True)


def unit_kernel(rows_ref, out_ref):
    v = rows_ref[...].astype(F32)
    out_ref[...] = (v / jnp.sqrt(jnp.sum(v * v, axis=1, keepdims=True) + 1e-06)).astype(BF)


def pairs_kernel(own, rows, par_ref, pos_ref, text_ref, image_ref, out_ref):
    text = text_ref[...]
    scores = lax.dot_general(
        image_ref[...], text, (((1,), (1,)), ((), ())), preferred_element_type=F32
    )
    logits = par_ref[0] * scores + par_ref[1]
    if own:
        a = lax.broadcasted_iota(jnp.int32, scores.shape, 1) - pos_ref[0]
        b = lax.broadcasted_iota(jnp.int32, scores.shape, 0) - pos_ref[1]
        sign = jnp.where((a == b) & (a >= 0) & (a < rows), -1.0, 1.0)
        pair = sign / (1.0 + jnp.exp(-sign * logits))
    else:
        pair = 1.0 / (1.0 + jnp.exp(-logits))
    pair = pair.astype(BF)
    dots = jnp.sum(pair.astype(F32) * scores, axis=1, keepdims=True)
    terms = jnp.dot(pair, text, preferred_element_type=F32)
    width = terms.shape[1]
    lane = lax.broadcasted_iota(jnp.int32, (terms.shape[0], 128), 1)
    if own:
        tail = jnp.where(lane == 0, dots, 0.0)
    else:
        high = dots.astype(BF).astype(F32)
        tail = jnp.where(lane == 0, high, jnp.where(lane == 1, dots - high, 0.0))
    out_ref[:width] = terms.T.astype(out_ref.dtype)
    out_ref[width:] = tail.T[:16].astype(out_ref.dtype)


def pairs(own, rows, par, pos, text, image):
    count, width = image.shape
    smem = pl.BlockSpec(memory_space=pltpu.SMEM)
    vmem = pl.BlockSpec(memory_space=pltpu.VMEM)
    return pl.pallas_call(
        lambda *refs: pairs_kernel(own, rows, *refs),
        in_specs=[smem, smem, vmem, vmem],
        out_specs=vmem,
        out_shape=jax.ShapeDtypeStruct((width + 16, count), F32 if own else BF),
        compiler_params=pltpu.CompilerParams(vmem_limit_bytes=40 * 2**20),
        cost_estimate=pl.CostEstimate(
            flops=4 * count * width * text.shape[0],
            bytes_accessed=2 * width * (text.shape[0] + 2 * count),
            transcendentals=count * text.shape[0],
        ),
        name="pairs_own" if own else "pairs_other",
    )(par, pos, text, image)


def join_kernel(own_ref, other_ref, out_ref):
    blocks, height, _ = out_ref.shape
    cols = height - 16
    total = own_ref[blocks * cols :] + other_ref[blocks * cols :].astype(F32)
    dots = total[0:1] + total[1:2]
    high = dots.astype(BF).astype(F32)
    row = lax.broadcasted_iota(jnp.int32, total.shape, 0)
    tail = jnp.where(row == 0, high, jnp.where(row == 1, dots - high, 0.0)).astype(BF)
    for t in range(blocks):
        part = pl.ds(t * cols, cols)
        out_ref[t, :cols] = (own_ref[part] + other_ref[part].astype(F32)).astype(BF)
        out_ref[t, cols:] = tail


def per_device(pooled, texts, head_w, log_scale, bias):
    z, yl, c = lax.axis_index("z"), lax.axis_index("yl"), lax.axis_index("c")
    yh, x = lax.axis_index("yh"), lax.axis_index("x")
    rows, width = pooled.shape
    cols = head_w.shape[0]
    scale = jnp.exp(log_scale[0])
    shift = bias[0]

    text_unit = pl.pallas_call(
        unit_kernel, out_shape=jax.ShapeDtypeStruct(texts.shape, BF), name="unit_texts"
    )(texts)
    text_pair = lax.all_gather(text_unit, "yl", axis=0, tiled=True)
    text_own = lax.all_gather(text_pair, "z", axis=0, tiled=True)

    images = gather_t(pooled)
    count = images.shape[0]
    own_cols = lax.dot_general(
        head_w, images, (((1,), (1,)), ((), ())), preferred_element_type=F32
    ).astype(BF)
    proj = gather_t(own_cols).reshape(NX, NYH, cols, count)
    proj = proj.transpose(1, 0, 2, 3).reshape(width, count)
    unit_all, norms = unit(proj, 0)
    embedded = unit_all.astype(BF).T
    embedded_other = lax.ppermute(embedded, "c", CORES)

    small = width // (NZ * NYL * NC)
    padded = -(-small // 16) * 16
    parts = images.T.reshape(NZ, NYL * NC, small, count).transpose(1, 0, 2, 3)
    parts = jnp.pad(parts, ((0, 0), (0, 0), (0, padded - small), (0, 0)))
    parts = lax.all_to_all(parts, ("yl", "c"), split_axis=0, concat_axis=0, tiled=True)

    text_own, embedded, embedded_other, norms, parts = lax.optimization_barrier(
        (text_own, embedded, embedded_other, norms, parts)
    )
    par = jnp.stack([scale, shift])
    pos = jnp.stack([(z * NYL + yl) * rows, (x * NYH + yh) * rows]).astype(jnp.int32)
    terms_other = pairs(False, rows, par, pos, text_own, embedded_other)
    terms_other = lax.ppermute(terms_other, "c", CORES)
    terms_own = pairs(True, rows, par, pos, text_own, embedded)
    block = pl.pallas_call(
        join_kernel,
        out_shape=jax.ShapeDtypeStruct((NYH * NX, cols + 16, count), BF),
        compiler_params=pltpu.CompilerParams(vmem_limit_bytes=40 * 2**20),
        name="join_cores",
    )(terms_own, terms_other)
    block = lax.all_to_all(block, T, split_axis=0, concat_axis=0, tiled=True)
    block = scale * jnp.sum(block.astype(F32), axis=0)
    row_dots = block[cols : cols + 1] + block[cols + 1 : cols + 2]
    own_unit = own_cols.astype(F32) / norms
    grad_proj = ((block[:cols] - own_unit * row_dots) / norms).astype(BF)

    grad_pooled = lax.dot_general(
        grad_proj, head_w, (((0,), (0,)), ((), ())), preferred_element_type=F32
    ).astype(BF)
    grad_pooled = grad_pooled.reshape(NX * NYH, rows, width)
    grad_pooled = lax.all_to_all(grad_pooled, ("x", "yh"), split_axis=0, concat_axis=0, tiled=True)
    grad_pooled = jnp.sum(grad_pooled.astype(F32), axis=0)

    grad_all = lax.all_gather(grad_proj, ("yl", "c"), axis=0)
    grad_head = jnp.einsum("szri,sfi->zrf", parts, grad_all, preferred_element_type=F32).astype(BF)
    grad_head = lax.all_to_all(grad_head, "z", split_axis=0, concat_axis=0, tiled=True)
    grad_head = jnp.sum(grad_head.astype(F32), axis=0)[:small]
    return (grad_pooled, grad_head)


def solution(mesh):
    fine = Mesh(mesh.devices.reshape(NZ, NYL, NC, NYH, NX), ("z", "yl", "c", "yh", "x"))
    dp = ("z", "yl", "c")
    rows = P(dp + T, None)
    return jax.shard_map(
        per_device,
        mesh=fine,
        in_specs=(rows, rows, P(T, None), P(), P()),
        out_specs=(rows, P(dp, T)),
        check_vma=False,
    )
```

time: 247 us -> 191 us (0.77)
  waiting for transfers between devices: 107 us -> 34.1 us
  matrix products: 15.8 us -> 4.23 us
  starting transfers between devices: 14.1 us -> 24.3 us
  local copies, waits for them, and re-layouts: 3.44 us -> 13.3 us
  Pallas kernels: 0 us -> 7.69 us
  blocking collectives: 81.7 us -> 87 us
  other arithmetic: 6.61 us -> 3.8 us
    all_gather x1, waiting for transfers between devices: 81.8 us -> 4.76 us  [per_device(): text_own = lax.all_gather(text_pair, 'z', axis=0, tiled=True)]
    dot_general x4 -> x0, matrix products: 12.8 us -> none  [the longest x2 7.23 us: half(): lax.dot_general(text, pair, (((0,), (0,)), ((), ())), preferred_element_t...]
    all_to_all x1, waiting for transfers between devices: 0.01 us -> 11.4 us  [per_device(): lax.all_to_all(parts, ('yl', 'c'), split_axis=0, concat_axis=0, tiled=True)]
    pallas_call x0 -> x4, Pallas kernels: none -> 7.69 us  [the longest x2 5.8 us: pairs(): pl.pallas_call(lambda *refs: pairs_kernel(own, rows, *refs), in_specs=[sm...]
    all_to_all x0 -> x1, starting transfers between devices: none -> 6.42 us  [per_device(): lax.all_to_all(grad_pooled, ('x', 'yh'), split_axis=0, concat_axis=0, til...]
    reduce_scatter x2 -> x0, waiting for transfers between devices: 6.1 us -> none  [the longest x1 6.08 us: per_device(): lax.psum_scatter(grad_pooled, 'yh', scatter_dimension=0, tiled=True)]
    unnamed x5 -> x13, local copies, waits for them, and re-layouts: 0.1 us -> 4.58 us
    convert_element_type x4 -> x0, other arithmetic: 4.26 us -> none  [the longest x1 1.65 us: per_device(): embedded = unit_all.astype(BF)]
  transfers between devices with their start and end apart: 6 -> 6, of which waited for: 3 -> 3; matrix products, arithmetic and copies ran while one was open for 5% -> 8% of each run, Pallas kernels for 0% -> 2%
where the time goes in v3:
time: 191 us; the launch traced here: 190 us
  blocking collectives  87 us (46%)
  waiting for transfers between devices  34.1 us (18%)
  starting transfers between devices  24.3 us (13%)
  between operations  15.5 us (8%)
  local copies, waits for them, and re-layouts  13.3 us (7%)
  Pallas kernels  7.69 us (4%)
  matrix products  4.23 us (2%)
  other arithmetic  3.8 us (2%)
    all_gather x2, blocking collectives, gather_t(): lax.all_gather(lax.all_gather(v, 'yh', axis=0, tiled=True), 'x', axis=0,...  28.1 us
    all_to_all x1, blocking collectives, per_device(): block = lax.all_to_all(block, T, split_axis=0, concat_axis=0, tiled=True)  21.4 us
    all_to_all x1, waiting for transfers between devices, per_device(): lax.all_to_all(grad_head, 'z', split_axis=0, concat_axis=0, tiled=True)  17.9 us
    all_gather x2, blocking collectives, gather_t(): lax.all_gather(v, 'yh', axis=0, tiled=True)  16.6 us
    all_gather x1, blocking collectives, per_device(): grad_all = lax.all_gather(grad_proj, ('yl', 'c'), axis=0)  14.5 us
    all_to_all x1, waiting for transfers between devices, per_device(): lax.all_to_all(parts, ('yl', 'c'), split_axis=0, concat_axis=0, tiled=True)  11.4 us
    all_to_all x1, starting transfers between devices, per_device(): lax.all_to_all(grad_head, 'z', split_axis=0, concat_axis=0, tiled=True)  9.61 us
    all_to_all x1, starting transfers between devices, per_device(): lax.all_to_all(grad_pooled, ('x', 'yh'), split_axis=0, concat_axis=0, til...  6.42 us
  transfers between devices with their start and end apart: 6, of which 3 were waited for; matrix products, arithmetic and copies ran while one was open for 8% of the time, Pallas kernels for 2%

profile of v3, /device:TPU:24, one launch (start us, length us, event | category | flops | bytes accessed | tf_op | source)
XLA Modules:
  0.0 189.9 jit_solution(4690953809494174985)
XLA Ops:
  7.2 1.7 unit_texts.1
  9.0 6.4 %all_gather.24 = bf16[64,1792]{1,0:T(8,128)(2,1)} all-gather(bf16[32,1792]{1,0:T(8,128)(2,1)} %unit_texts.1), channel_id=1, replica_groups=mesh['z'=16,'yl'=2,'c'=2,'yh'=2,'x'=4] {'yl'}, dimensions={0}, use_global_device_ids=true | all-gather | bytes 344064 | tf_op jit(solution)/shard_map/all_gather | solution.py:101
  15.4 9.6 %all_gather.26 = bf16[64,1792]{1,0:T(8,128)(2,1)S(1)} all-gather(bf16[32,1792]{1,0:T(8,128)(2,1)} %param.5), channel_id=1, replica_groups=mesh['z'=16,'yl'=2,'c'=2,'yh'=2,'x'=4] {'yh'}, dimensions={0}, use_global_device_ids=true | all-gather | bytes 344064 | tf_op jit(solution)/shard_map/all_gather | solution.py:22
  25.0 14.6 %all_gather.27 = bf16[256,1792]{1,0:T(8,128)(2,1)S(1)} all-gather(bf16[64,1792]{1,0:T(8,128)(2,1)S(1)} %all_gather.26), channel_id=1, replica_groups=mesh['z'=16,'yl'=2,'c'=2,'yh'=2,'x'=4] {'x'}, dimensions={0}, use_global_device_ids=true | all-gather | bytes 1146880 | tf_op jit(solution)/shard_map/all_gather | solution.py:22
  40.0 0.6 copy-done.2
  40.7 7.0 %all_gather.28 = bf16[448,256]{1,0:T(8,128)(2,1)S(1)} all-gather(bf16[224,256]{1,0:T(8,128)(2,1)S(1)} %convolution_convert_fusion.1), channel_id=1, replica_groups=mesh['z'=16,'yl'=2,'c'=2,'yh'=2,'x'=4] {'yh'}, dimensions={0}, use_global_device_ids=true | all-gather | bytes 344064 | tf_op jit(solution)/shard_map/all_gather | solution.py:22
  47.6 13.6 %all_gather.29 = bf16[1792,256]{1,0:T(8,128)(2,1)S(1)} all-gather(bf16[448,256]{1,0:T(8,128)(2,1)S(1)} %all_gather.28), channel_id=1, replica_groups=mesh['z'=16,'yl'=2,'c'=2,'yh'=2,'x'=4] {'x'}, dimensions={0}, use_global_device_ids=true | all-gather | bytes 1146880 | tf_op jit(solution)/shard_map/all_gather | solution.py:22
  61.2 1.4 copy.12
  62.6 2.7 %copy.13 = f32[1792,256]{0,1:T(8,128)} copy(f32[1792,256]{1,0:T(8,128)} %bitcast.34) | data formatting | bytes 3670016 | tf_op jit(solution)/shard_map/convert_element_type | solution.py:16
  65.6 0.6 copy-done.4
  66.2 1.7 fusion.1.refs_3_
  67.9 1.9 %collective-permute-start = (bf16[256,1792]{1,0:T(8,128)(2,1)S(1)}, bf16[256,1792]{1,0:T(8,128)(2,1)S(1)}, u32[]{:S(2)}, u32[]{:S(2)}) collective-permute-start(bf16[256,1792]{1,0:T(8,128)(2,1)S(1)} %fusion.1.refs_3_), channel_id=1, source_target_pairs={{0,8},{8,0},{1,9},{9,1},{2,10},{10,2},{3,11},{11,3},{4,12},{12,4},... | collective-permute-start | bytes 2752520 | tf_op jit(solution)/shard_map/ppermute | solution.py:113
  69.8 1.3 copy.14
  71.1 2.1 %reshape.35 = bf16[16,4,28,256]{3,2,1,0:T(8,128)(2,1)} reshape(bf16[1792,256]{1,0:T(8,128)(2,1)} %copy.14) | data formatting | bytes 1835008 | tf_op jit(solution)/shard_map/reshape | solution.py:117
  73.3 1.3 copy.19
  74.6 1.1 pad.4.clone
  75.7 4.4 %all-to-all-start = ((bf16[4,16,32,256]{3,2,1,0:T(8,128)(2,1)}), bf16[4,16,32,256]{3,2,1,0:T(8,128)(2,1)}, u32[]{:S(2)}, u32[]{:S(2)}) async-start(bf16[4,16,32,256]{3,2,1,0:T(8,128)(2,1)} %pad.4.clone), calls=%async_computation | async-start | bytes 2097152 | tf_op jit(solution)/shard_map/all_to_all | solution.py:119
  81.6 11.4 %all-to-all-done = bf16[4,16,32,256]{3,2,1,0:T(8,128)(2,1)} async-done(((bf16[4,16,32,256]{3,2,1,0:T(8,128)(2,1)}), bf16[4,16,32,256]{3,2,1,0:T(8,128)(2,1)}, u32[]{:S(2)}, u32[]{:S(2)}) %all-to-all-start) | async-done | bytes 1048608 | tf_op jit(solution)/shard_map/all_to_all | solution.py:119
  93.0 4.8 %all-gather.3.cloned.1.call-done.refs_2_ = bf16[1024,1792]{1,0:T(8,128)(2,1)} async-done(((bf16[64,1792]{1,0:T(8,128)(2,1)}), bf16[1024,1792]{1,0:T(8,128)(2,1)}) %all-gather.3.cloned.1.call-update) | async-done | bytes 3670032 | tf_op jit(solution)/shard_map/all_gather | solution.py:102
  97.8 2.0 %copy-done.1 = bf16[1024,1792]{1,0:T(8,128)(2,1)S(1)} copy-done((bf16[1024,1792]{1,0:T(8,128)(2,1)S(1)}, bf16[1024,1792]{1,0:T(8,128)(2,1)}, u32[]{:S(2)}) %copy-start.1) | copy-done | bytes 3670040
  99.8 2.9 %pairs_other.1 = bf16[1808,256]{1,0:T(8,128)(2,1)S(1)} custom-call(f32[2]{0:T(128)S(1)} %pad_maximum_fusion.refs_0_, s32[2]{0:T(128)S(1)} %pad_add_fusion.refs_1_, bf16[1024,1792]{1,0:T(8,128)(2,1)S(1)} %copy-done.1, bf16[256,1792]{1,0:T(8,128)(2,1)S(1)} %collective-permute-done.refs_3_), custom_call_target="tpu_custom_call" | custom-call | flops 1879048192 | bytes 5505024 | tf_op jit(solution)/shard_map/pairs_other/pallas_call | solution.py:61
  102.7 1.9 %collective-permute-start.1 = (bf16[1808,256]{1,0:T(8,128)(2,1)S(1)}, bf16[1808,256]{1,0:T(8,128)(2,1)S(1)}, u32[]{:S(2)}, u32[]{:S(2)}) collective-permute-start(bf16[1808,256]{1,0:T(8,128)(2,1)S(1)} %pairs_other.1), channel_id=1, source_target_pairs={{0,8},{8,0},{1,9},{9,1},{2,10},{10,2},{3,11},{11,3},{4,12},{12,4},... | collective-permute-start | bytes 2777096 | tf_op jit(solution)/shard_map/ppermute | solution.py:127
  104.6 2.9 %pairs_own.1.own_ref = f32[1808,256]{1,0:T(8,128)S(1)} custom-call(f32[2]{0:T(128)S(1)} %pad_maximum_fusion.refs_0_, s32[2]{0:T(128)S(1)} %pad_add_fusion.refs_1_, bf16[1024,1792]{1,0:T(8,128)(2,1)S(1)} %copy-done.1, bf16[256,1792]{1,0:T(8,128)(2,1)S(1)} %fusion.1.refs_3_), custom_call_target="tpu_custom_call" | custom-call | flops 1879048192 | bytes 5505024 | tf_op jit(solution)/shard_map/pairs_own/pallas_call | solution.py:61
  107.7 21.4 %all_to_all.20 = bf16[8,240,256]{2,1,0:T(8,128)(2,1)S(1)} all-to-all(bf16[8,240,256]{2,1,0:T(8,128)(2,1)S(1)} %join_cores.1), channel_id=1, replica_groups=mesh['z'=16,'yl'=2,'c'=2,'yh'=2,'x'=4] {'yh','x'}, dimensions={0} | all-to-all | bytes 1966080 | tf_op jit(solution)/shard_map/all_to_all | solution.py:135
  129.4 1.4 convolution_convert_fusion
  130.8 6.4 %all-to-all-start.2 = ((bf16[8,32,1792]{2,1,0:T(8,128)(2,1)}), bf16[8,32,1792]{2,1,0:T(8,128)(2,1)S(1)}, u32[]{:S(2)}, u32[]{:S(2)}) async-start(bf16[8,32,1792]{2,1,0:T(8,128)(2,1)} %bitcast.12), calls=%async_computation.2 | async-start | bytes 1835008 | tf_op jit(solution)/shard_map/all_to_all | solution.py:145
  137.2 14.5 %all-gather = bf16[896,256]{1,0:T(8,128)(2,1)S(1)} all-gather(bf16[224,256]{1,0:T(8,128)(2,1)S(1)} %fusion.3), channel_id=2, replica_groups=mesh['z'=16,'yl'=2,'c'=2,'yh'=2,'x'=4] {'yl','c'}, dimensions={0}, use_global_device_ids=true | all-gather | bytes 573440 | tf_op jit(solution)/shard_map/all_gather | solution.py:148
  151.7 2.4 %fusion = bf16[16,32,224]{2,1,0:T(8,128)(2,1)} fusion(bf16[4,16,32,256]{3,2,1,0:T(8,128)(2,1)} %all-to-all-done, bf16[4,224,256,1]{2,1,3,0:T(8,128)(2,1)S(1)} %bitcast.36), kind=kOutput, calls=%fused_computation.6 | convolution fusion | flops 234995712 | bytes 1736704 | tf_op jit(solution)/shard_map/szri,sfi->zrf/dot_general | solution.py:149
  154.1 9.6 %all-to-all-start.3 = ((bf16[16,32,224]{2,1,0:T(8,128)(2,1)}), bf16[16,32,224]{2,1,0:T(8,128)(2,1)S(1)}, u32[]{:S(2)}, u32[]{:S(2)}) async-start(bf16[16,32,224]{2,1,0:T(8,128)(2,1)} %fusion), calls=%async_computation.3 | async-start | bytes 524288 | tf_op jit(solution)/shard_map/all_to_all | solution.py:150
  163.7 0.8 convert_reduce_fusion.1
  164.5 17.9 %all-to-all-done.3 = bf16[16,32,224]{2,1,0:T(8,128)(2,1)S(1)} async-done(((bf16[16,32,224]{2,1,0:T(8,128)(2,1)}), bf16[16,32,224]{2,1,0:T(8,128)(2,1)S(1)}, u32[]{:S(2)}, u32[]{:S(2)}) %all-to-all-start.3) | async-done | bytes 229408 | tf_op jit(solution)/shard_map/all_to_all | solution.py:150
  182.4 0.7 convert_reduce_fusion.2
  (24 shorter events, 1.3 us)
Async XLA Ops:
  7.2 32.4 %copy-start = (bf16[224,1792]{1,0:T(8,128)(2,1)S(1)}, bf16[224,1792]{1,0:T(8,128)(2,1)}, u32[]{:S(2)}) copy-start(bf16[224,1792]{1,0:T(8,128)(2,1)} %param.7) | copy-start | bytes 2408452
  7.2 90.6 %all-gather.3.cloned.1.call-start = ((), (), s32[]{:S(2)}) async-start(), calls=%async_computation.4 | async-start | bytes 3899392 | tf_op jit(solution)/shard_map/all_gather | solution.py:102
  40.0 0.6 copy-start.2
  65.6 0.6 copy-start.4
  67.9 25.1 %collective-permute-start = (bf16[256,1792]{1,0:T(8,128)(2,1)S(1)}, bf16[256,1792]{1,0:T(8,128)(2,1)S(1)}, u32[]{:S(2)}, u32[]{:S(2)}) collective-permute-start(bf16[256,1792]{1,0:T(8,128)(2,1)S(1)} %fusion.1.refs_3_), channel_id=1, source_target_pairs={{0,8},{8,0},{1,9},{9,1},{2,10},{10,2},{3,11},{11,3},{4,12},{12,4},... | collective-permute-start | bytes 2752520 | tf_op jit(solution)/shard_map/ppermute | solution.py:113
  75.7 17.3 %all-to-all-start = ((bf16[4,16,32,256]{3,2,1,0:T(8,128)(2,1)}), bf16[4,16,32,256]{3,2,1,0:T(8,128)(2,1)}, u32[]{:S(2)}, u32[]{:S(2)}) async-start(bf16[4,16,32,256]{3,2,1,0:T(8,128)(2,1)} %pad.4.clone), calls=%async_computation | async-start | bytes 2097152 | tf_op jit(solution)/shard_map/all_to_all | solution.py:119
  97.8 2.0 %copy-start.1 = (bf16[1024,1792]{1,0:T(8,128)(2,1)S(1)}, bf16[1024,1792]{1,0:T(8,128)(2,1)}, u32[]{:S(2)}) copy-start(bf16[1024,1792]{1,0:T(8,128)(2,1)} %all-gather.3.cloned.1.call-done.refs_2_) | copy-start | bytes 11010052
  102.7 4.9 %collective-permute-start.1 = (bf16[1808,256]{1,0:T(8,128)(2,1)S(1)}, bf16[1808,256]{1,0:T(8,128)(2,1)S(1)}, u32[]{:S(2)}, u32[]{:S(2)}) collective-permute-start(bf16[1808,256]{1,0:T(8,128)(2,1)S(1)} %pairs_other.1), channel_id=1, source_target_pairs={{0,8},{8,0},{1,9},{9,1},{2,10},{10,2},{3,11},{11,3},{4,12},{12,4},... | collective-permute-start | bytes 2777096 | tf_op jit(solution)/shard_map/ppermute | solution.py:127
  107.7 21.6 %copy-start.3 = (bf16[224,256]{1,0:T(8,128)(2,1)S(1)}, bf16[224,256]{1,0:T(8,128)(2,1)}, u32[]{:S(2)}) copy-start(bf16[224,256]{1,0:T(8,128)(2,1)} %copy-done.2) | copy-start | bytes 344068
  107.7 21.6 %copy-start.5 = (f32[256]{0:T(256)S(1)}, f32[256]{0:T(256)}, u32[]{:S(2)}) copy-start(f32[256]{0:T(256)} %copy-done.4) | copy-start | bytes 3076
  130.8 23.3 %all-to-all-start.2 = ((bf16[8,32,1792]{2,1,0:T(8,128)(2,1)}), bf16[8,32,1792]{2,1,0:T(8,128)(2,1)S(1)}, u32[]{:S(2)}, u32[]{:S(2)}) async-start(bf16[8,32,1792]{2,1,0:T(8,128)(2,1)} %bitcast.12), calls=%async_computation.2 | async-start | bytes 1835008 | tf_op jit(solution)/shard_map/all_to_all | solution.py:145
  154.1 28.3 %all-to-all-start.3 = ((bf16[16,32,224]{2,1,0:T(8,128)(2,1)}), bf16[16,32,224]{2,1,0:T(8,128)(2,1)S(1)}, u32[]{:S(2)}, u32[]{:S(2)}) async-start(bf16[16,32,224]{2,1,0:T(8,128)(2,1)} %fusion), calls=%async_computation.3 | async-start | bytes 524288 | tf_op jit(solution)/shard_map/all_to_all | solution.py:150
Sparse Core Ops, SparseCore 0:
  15.5 82.2 all-gather.2

commit v4 on v3

--- a/solution.py
+++ b/solution.py
@@ -141,9 +141,11 @@
     grad_pooled = lax.dot_general(
         grad_proj, head_w, (((0,), (0,)), ((), ())), preferred_element_type=F32
     ).astype(BF)
-    grad_pooled = grad_pooled.reshape(NX * NYH, rows, width)
-    grad_pooled = lax.all_to_all(grad_pooled, ("x", "yh"), split_axis=0, concat_axis=0, tiled=True)
-    grad_pooled = jnp.sum(grad_pooled.astype(F32), axis=0)
+    grad_pooled = lax.psum_scatter(grad_pooled, "x", scatter_dimension=0, tiled=True)
+    given = jnp.where(yh == 0, grad_pooled[rows:], grad_pooled[:rows])
+    taken = lax.ppermute(given, "yh", CORES)
+    kept = jnp.where(yh == 0, grad_pooled[:rows], grad_pooled[rows:])
+    grad_pooled = kept.astype(F32) + taken.astype(F32)
 
     grad_all = lax.all_gather(grad_proj, ("yl", "c"), axis=0)
     grad_head = jnp.einsum("szri,sfi->zrf", parts, grad_all, preferred_element_type=F32).astype(BF)

time: 191 us -> 180 us (0.942); the launches traced: 190 us -> 177 us
  blocking collectives: 87 us -> 78.8 us
  starting transfers between devices: 24.3 us -> 20.9 us
  waiting for transfers between devices: 34.1 us -> 30.7 us
    all_to_all x1, waiting for transfers between devices: 17.9 us -> 4.68 us  [per_device(): lax.all_to_all(grad_head, 'z', split_axis=0, concat_axis=0, tiled=True)]
    reduce_scatter x0 -> x1, waiting for transfers between devices: none -> 9.8 us  [per_device(): lax.psum_scatter(grad_pooled, 'x', scatter_dimension=0, tiled=True)]
    all_gather x1, blocking collectives: 14.5 us -> 6.33 us  [per_device(): grad_all = lax.all_gather(grad_proj, ('yl', 'c'), axis=0)]
    all_to_all x1 -> x0, starting transfers between devices: 6.42 us -> none  [per_device(): lax.all_to_all(grad_pooled, ('x', 'yh'), split_axis=0, concat_axis=0, til...]
    ppermute x0 -> x1, starting transfers between devices: none -> 3.25 us  [per_device(): taken = lax.ppermute(given, 'yh', CORES)]
  transfers between devices with their start and end apart: 6 -> 7, of which waited for: 3 -> 4; matrix products, arithmetic and copies ran while one was open for 8% -> 9% of each run, Pallas kernels for 2% -> 2%
where the time goes in v4:
time: 180 us; the launch traced here: 177 us
  blocking collectives  78.8 us (44%)
  waiting for transfers between devices  30.7 us (17%)
  starting transfers between devices  20.9 us (12%)
  between operations  15.5 us (9%)
  local copies, waits for them, and re-layouts  13.3 us (7%)
  Pallas kernels  7.68 us (4%)
  other arithmetic  5.64 us (3%)
  matrix products  4.24 us (2%)
    all_gather x2, blocking collectives, gather_t(): lax.all_gather(lax.all_gather(v, 'yh', axis=0, tiled=True), 'x', axis=0,...  28.1 us
    all_to_all x1, blocking collectives, per_device(): block = lax.all_to_all(block, T, split_axis=0, concat_axis=0, tiled=True)  21.4 us
    all_gather x2, blocking collectives, gather_t(): lax.all_gather(v, 'yh', axis=0, tiled=True)  16.6 us
    all_to_all x1, waiting for transfers between devices, per_device(): lax.all_to_all(parts, ('yl', 'c'), split_axis=0, concat_axis=0, tiled=True)  11.4 us
    reduce_scatter x1, waiting for transfers between devices, per_device(): lax.psum_scatter(grad_pooled, 'x', scatter_dimension=0, tiled=True)  9.8 us
    all_to_all x1, starting transfers between devices, per_device(): lax.all_to_all(grad_head, 'z', split_axis=0, concat_axis=0, tiled=True)  9.43 us
    all_gather x1, blocking collectives, per_device(): text_pair = lax.all_gather(text_unit, 'yl', axis=0, tiled=True)  6.38 us
    all_gather x1, blocking collectives, per_device(): grad_all = lax.all_gather(grad_proj, ('yl', 'c'), axis=0)  6.33 us
  transfers between devices with their start and end apart: 7, of which 4 were waited for; matrix products, arithmetic and copies ran while one was open for 9% of the time, Pallas kernels for 2%

profile of v4, /device:TPU:24, one launch (start us, length us, event | category | flops | bytes accessed | tf_op | source)
XLA Modules:
  0.0 176.9 jit_solution(3798996565034536593)
XLA Ops:
  7.2 1.7 unit_texts.1
  9.0 6.4 %all_gather.24 = bf16[64,1792]{1,0:T(8,128)(2,1)} all-gather(bf16[32,1792]{1,0:T(8,128)(2,1)} %unit_texts.1), channel_id=1, replica_groups=mesh['z'=16,'yl'=2,'c'=2,'yh'=2,'x'=4] {'yl'}, dimensions={0}, use_global_device_ids=true | all-gather | bytes 344064 | tf_op jit(solution)/shard_map/all_gather | solution.py:101
  15.4 9.6 %all_gather.26 = bf16[64,1792]{1,0:T(8,128)(2,1)S(1)} all-gather(bf16[32,1792]{1,0:T(8,128)(2,1)} %param.5), channel_id=1, replica_groups=mesh['z'=16,'yl'=2,'c'=2,'yh'=2,'x'=4] {'yh'}, dimensions={0}, use_global_device_ids=true | all-gather | bytes 344064 | tf_op jit(solution)/shard_map/all_gather | solution.py:22
  25.0 14.6 %all_gather.27 = bf16[256,1792]{1,0:T(8,128)(2,1)S(1)} all-gather(bf16[64,1792]{1,0:T(8,128)(2,1)S(1)} %all_gather.26), channel_id=1, replica_groups=mesh['z'=16,'yl'=2,'c'=2,'yh'=2,'x'=4] {'x'}, dimensions={0}, use_global_device_ids=true | all-gather | bytes 1146880 | tf_op jit(solution)/shard_map/all_gather | solution.py:22
  40.7 7.0 %all_gather.28 = bf16[448,256]{1,0:T(8,128)(2,1)S(1)} all-gather(bf16[224,256]{1,0:T(8,128)(2,1)S(1)} %convolution_convert_fusion.1), channel_id=1, replica_groups=mesh['z'=16,'yl'=2,'c'=2,'yh'=2,'x'=4] {'yh'}, dimensions={0}, use_global_device_ids=true | all-gather | bytes 344064 | tf_op jit(solution)/shard_map/all_gather | solution.py:22
  47.6 13.6 %all_gather.29 = bf16[1792,256]{1,0:T(8,128)(2,1)S(1)} all-gather(bf16[448,256]{1,0:T(8,128)(2,1)S(1)} %all_gather.28), channel_id=1, replica_groups=mesh['z'=16,'yl'=2,'c'=2,'yh'=2,'x'=4] {'x'}, dimensions={0}, use_global_device_ids=true | all-gather | bytes 1146880 | tf_op jit(solution)/shard_map/all_gather | solution.py:22
  61.2 1.4 copy.12
  62.6 2.7 %copy.13 = f32[1792,256]{0,1:T(8,128)} copy(f32[1792,256]{1,0:T(8,128)} %bitcast.33) | data formatting | bytes 3670016 | tf_op jit(solution)/shard_map/convert_element_type | solution.py:16
  66.2 1.7 fusion.1.refs_3_
  67.9 1.9 %collective-permute-start = (bf16[256,1792]{1,0:T(8,128)(2,1)S(1)}, bf16[256,1792]{1,0:T(8,128)(2,1)S(1)}, u32[]{:S(2)}, u32[]{:S(2)}) collective-permute-start(bf16[256,1792]{1,0:T(8,128)(2,1)S(1)} %fusion.1.refs_3_), channel_id=1, source_target_pairs={{0,8},{8,0},{1,9},{9,1},{2,10},{10,2},{3,11},{11,3},{4,12},{12,4},... | collective-permute-start | bytes 2752520 | tf_op jit(solution)/shard_map/ppermute | solution.py:113
  69.8 1.3 copy.14
  71.1 2.1 %reshape.32 = bf16[16,4,28,256]{3,2,1,0:T(8,128)(2,1)} reshape(bf16[1792,256]{1,0:T(8,128)(2,1)} %copy.14) | data formatting | bytes 1835008 | tf_op jit(solution)/shard_map/reshape | solution.py:117
  73.3 1.3 copy.19
  74.6 1.1 pad.4.clone
  75.7 4.4 %all-to-all-start = ((bf16[4,16,32,256]{3,2,1,0:T(8,128)(2,1)}), bf16[4,16,32,256]{3,2,1,0:T(8,128)(2,1)}, u32[]{:S(2)}, u32[]{:S(2)}) async-start(bf16[4,16,32,256]{3,2,1,0:T(8,128)(2,1)} %pad.4.clone), calls=%async_computation | async-start | bytes 2097152 | tf_op jit(solution)/shard_map/all_to_all | solution.py:119
  81.6 11.4 %all-to-all-done = bf16[4,16,32,256]{3,2,1,0:T(8,128)(2,1)} async-done(((bf16[4,16,32,256]{3,2,1,0:T(8,128)(2,1)}), bf16[4,16,32,256]{3,2,1,0:T(8,128)(2,1)}, u32[]{:S(2)}, u32[]{:S(2)}) %all-to-all-start) | async-done | bytes 1048608 | tf_op jit(solution)/shard_map/all_to_all | solution.py:119
  93.0 4.8 %all-gather.3.cloned.1.call-done.refs_2_ = bf16[1024,1792]{1,0:T(8,128)(2,1)} async-done(((bf16[64,1792]{1,0:T(8,128)(2,1)}), bf16[1024,1792]{1,0:T(8,128)(2,1)}) %all-gather.3.cloned.1.call-update) | async-done | bytes 3670032 | tf_op jit(solution)/shard_map/all_gather | solution.py:102
  97.8 2.0 %copy-done.1 = bf16[1024,1792]{1,0:T(8,128)(2,1)S(1)} copy-done((bf16[1024,1792]{1,0:T(8,128)(2,1)S(1)}, bf16[1024,1792]{1,0:T(8,128)(2,1)}, u32[]{:S(2)}) %copy-start.1) | copy-done | bytes 3670040
  99.8 2.9 %pairs_other.1 = bf16[1808,256]{1,0:T(8,128)(2,1)S(1)} custom-call(f32[2]{0:T(128)S(1)} %pad_maximum_fusion.refs_0_, s32[2]{0:T(128)S(1)} %pad_add_fusion.refs_1_, bf16[1024,1792]{1,0:T(8,128)(2,1)S(1)} %copy-done.1, bf16[256,1792]{1,0:T(8,128)(2,1)S(1)} %collective-permute-done.refs_3_), custom_call_target="tpu_custom_call" | custom-call | flops 1879048192 | bytes 5505024 | tf_op jit(solution)/shard_map/pairs_other/pallas_call | solution.py:61
  102.7 1.9 %collective-permute-start.1 = (bf16[1808,256]{1,0:T(8,128)(2,1)S(1)}, bf16[1808,256]{1,0:T(8,128)(2,1)S(1)}, u32[]{:S(2)}, u32[]{:S(2)}) collective-permute-start(bf16[1808,256]{1,0:T(8,128)(2,1)S(1)} %pairs_other.1), channel_id=1, source_target_pairs={{0,8},{8,0},{1,9},{9,1},{2,10},{10,2},{3,11},{11,3},{4,12},{12,4},... | collective-permute-start | bytes 2777096 | tf_op jit(solution)/shard_map/ppermute | solution.py:127
  104.6 2.9 %pairs_own.1.own_ref = f32[1808,256]{1,0:T(8,128)S(1)} custom-call(f32[2]{0:T(128)S(1)} %pad_maximum_fusion.refs_0_, s32[2]{0:T(128)S(1)} %pad_add_fusion.refs_1_, bf16[1024,1792]{1,0:T(8,128)(2,1)S(1)} %copy-done.1, bf16[256,1792]{1,0:T(8,128)(2,1)S(1)} %fusion.1.refs_3_), custom_call_target="tpu_custom_call" | custom-call | flops 1879048192 | bytes 5505024 | tf_op jit(solution)/shard_map/pairs_own/pallas_call | solution.py:61
  107.8 21.4 %all_to_all.15 = bf16[8,240,256]{2,1,0:T(8,128)(2,1)S(1)} all-to-all(bf16[8,240,256]{2,1,0:T(8,128)(2,1)S(1)} %join_cores.1), channel_id=1, replica_groups=mesh['z'=16,'yl'=2,'c'=2,'yh'=2,'x'=4] {'yh','x'}, dimensions={0} | all-to-all | bytes 1966080 | tf_op jit(solution)/shard_map/all_to_all | solution.py:135
  129.4 1.4 convolution_convert_fusion
  130.8 6.3 %all-gather = bf16[896,256]{1,0:T(8,128)(2,1)S(1)} all-gather(bf16[224,256]{1,0:T(8,128)(2,1)S(1)} %fusion.3), channel_id=2, replica_groups=mesh['z'=16,'yl'=2,'c'=2,'yh'=2,'x'=4] {'yl','c'}, dimensions={0}, use_global_device_ids=true | all-gather | bytes 573440 | tf_op jit(solution)/shard_map/all_gather | solution.py:150
  137.1 2.4 %fusion = bf16[16,32,224]{2,1,0:T(8,128)(2,1)} fusion(bf16[4,16,32,256]{3,2,1,0:T(8,128)(2,1)} %all-to-all-done, bf16[4,224,256,1]{2,1,3,0:T(8,128)(2,1)S(1)} %bitcast.35), kind=kOutput, calls=%fused_computation.5 | convolution fusion | flops 234995712 | bytes 1736704 | tf_op jit(solution)/shard_map/szri,sfi->zrf/dot_general | solution.py:151
  139.5 9.4 %all-to-all-start.2 = ((bf16[16,32,224]{2,1,0:T(8,128)(2,1)}), bf16[16,32,224]{2,1,0:T(8,128)(2,1)S(1)}, u32[]{:S(2)}, u32[]{:S(2)}) async-start(bf16[16,32,224]{2,1,0:T(8,128)(2,1)} %fusion), calls=%async_computation.3 | async-start | bytes 524288 | tf_op jit(solution)/shard_map/all_to_all | solution.py:152
  149.0 9.8 %reduce-scatter.2.cloned.1.call-done = bf16[64,1792]{1,0:T(8,128)(2,1)} async-done(((bf16[256,1792]{1,0:T(8,128)(2,1)}), bf16[64,1792]{1,0:T(8,128)(2,1)}) %reduce-scatter.2.cloned.1.call-update) | async-done | bytes 229392 | tf_op jit(solution)/shard_map/reduce_scatter | solution.py:144
  158.8 1.0 broadcast_select_fusion
  159.8 3.3 %collective-permute-start.2 = (bf16[32,1792]{1,0:T(8,128)(2,1)S(1)}, bf16[32,1792]{1,0:T(8,128)(2,1)S(1)}, u32[]{:S(2)}, u32[]{:S(2)}) collective-permute-start(bf16[32,1792]{1,0:T(8,128)(2,1)S(1)} %broadcast_select_fusion), channel_id=1, source_target_pairs={{0,4},{4,0},{1,5},{5,1},{2,6},{6,2},{3,7},{7,3},{8,12},{12,8},{9,1... | collective-permute-start | bytes 344072 | tf_op jit(solution)/shard_map/ppermute | solution.py:146
  163.0 4.7 %all-to-all-done.2 = bf16[16,32,224]{2,1,0:T(8,128)(2,1)S(1)} async-done(((bf16[16,32,224]{2,1,0:T(8,128)(2,1)}), bf16[16,32,224]{2,1,0:T(8,128)(2,1)S(1)}, u32[]{:S(2)}, u32[]{:S(2)}) %all-to-all-start.2) | async-done | bytes 229408 | tf_op jit(solution)/shard_map/all_to_all | solution.py:152
  167.7 0.7 convert_reduce_fusion.1
  168.4 1.7 convert_add_fusion
  (28 shorter events, 2.6 us)
Async XLA Ops:
  7.2 32.4 %copy-start = (bf16[224,1792]{1,0:T(8,128)(2,1)S(1)}, bf16[224,1792]{1,0:T(8,128)(2,1)}, u32[]{:S(2)}) copy-start(bf16[224,1792]{1,0:T(8,128)(2,1)} %param.7) | copy-start | bytes 2408452
  7.2 90.6 %all-gather.3.cloned.1.call-start = ((), (), s32[]{:S(2)}) async-start(), calls=%async_computation.4 | async-start | bytes 3899392 | tf_op jit(solution)/shard_map/all_gather | solution.py:102
  40.0 0.6 copy-start.2
  65.6 0.6 copy-start.4
  67.9 25.1 %collective-permute-start = (bf16[256,1792]{1,0:T(8,128)(2,1)S(1)}, bf16[256,1792]{1,0:T(8,128)(2,1)S(1)}, u32[]{:S(2)}, u32[]{:S(2)}) collective-permute-start(bf16[256,1792]{1,0:T(8,128)(2,1)S(1)} %fusion.1.refs_3_), channel_id=1, source_target_pairs={{0,8},{8,0},{1,9},{9,1},{2,10},{10,2},{3,11},{11,3},{4,12},{12,4},... | collective-permute-start | bytes 2752520 | tf_op jit(solution)/shard_map/ppermute | solution.py:113
  75.7 17.3 %all-to-all-start = ((bf16[4,16,32,256]{3,2,1,0:T(8,128)(2,1)}), bf16[4,16,32,256]{3,2,1,0:T(8,128)(2,1)}, u32[]{:S(2)}, u32[]{:S(2)}) async-start(bf16[4,16,32,256]{3,2,1,0:T(8,128)(2,1)} %pad.4.clone), calls=%async_computation | async-start | bytes 2097152 | tf_op jit(solution)/shard_map/all_to_all | solution.py:119
  80.1 78.7 %reduce-scatter.2.cloned.1.call-start = ((), (), s32[]{:S(2)}) async-start(), calls=%async_computation.5 | async-start | bytes 1146880 | tf_op jit(solution)/shard_map/reduce_scatter | solution.py:144
  97.8 2.0 %copy-start.1 = (bf16[1024,1792]{1,0:T(8,128)(2,1)S(1)}, bf16[1024,1792]{1,0:T(8,128)(2,1)}, u32[]{:S(2)}) copy-start(bf16[1024,1792]{1,0:T(8,128)(2,1)} %all-gather.3.cloned.1.call-done.refs_2_) | copy-start | bytes 11010052
  102.7 4.9 %collective-permute-start.1 = (bf16[1808,256]{1,0:T(8,128)(2,1)S(1)}, bf16[1808,256]{1,0:T(8,128)(2,1)S(1)}, u32[]{:S(2)}, u32[]{:S(2)}) collective-permute-start(bf16[1808,256]{1,0:T(8,128)(2,1)S(1)} %pairs_other.1), channel_id=1, source_target_pairs={{0,8},{8,0},{1,9},{9,1},{2,10},{10,2},{3,11},{11,3},{4,12},{12,4},... | collective-permute-start | bytes 2777096 | tf_op jit(solution)/shard_map/ppermute | solution.py:127
  107.7 21.6 %copy-start.3 = (bf16[224,256]{1,0:T(8,128)(2,1)S(1)}, bf16[224,256]{1,0:T(8,128)(2,1)}, u32[]{:S(2)}) copy-start(bf16[224,256]{1,0:T(8,128)(2,1)} %copy-done.2) | copy-start | bytes 344068
  107.7 21.6 %copy-start.5 = (f32[256]{0:T(256)S(1)}, f32[256]{0:T(256)}, u32[]{:S(2)}) copy-start(f32[256]{0:T(256)} %copy-done.4) | copy-start | bytes 3076
  139.5 28.2 %all-to-all-start.2 = ((bf16[16,32,224]{2,1,0:T(8,128)(2,1)}), bf16[16,32,224]{2,1,0:T(8,128)(2,1)S(1)}, u32[]{:S(2)}, u32[]{:S(2)}) async-start(bf16[16,32,224]{2,1,0:T(8,128)(2,1)} %fusion), calls=%async_computation.3 | async-start | bytes 524288 | tf_op jit(solution)/shard_map/all_to_all | solution.py:152
  159.8 8.6 %collective-permute-start.2 = (bf16[32,1792]{1,0:T(8,128)(2,1)S(1)}, bf16[32,1792]{1,0:T(8,128)(2,1)S(1)}, u32[]{:S(2)}, u32[]{:S(2)}) collective-permute-start(bf16[32,1792]{1,0:T(8,128)(2,1)S(1)} %broadcast_select_fusion), channel_id=1, source_target_pairs={{0,4},{4,0},{1,5},{5,1},{2,6},{6,2},{3,7},{7,3},{8,12},{12,8},{9,1... | collective-permute-start | bytes 344072 | tf_op jit(solution)/shard_map/ppermute | solution.py:146
Sparse Core Ops, SparseCore 0:
  15.5 82.2 all-gather.2
  130.9 27.8 reduce-scatter.1

commit v5 on v4

--- a/solution.py
+++ b/solution.py
@@ -73,6 +73,19 @@
     )(par, pos, text, image)
 
 
+def score(image, text):
+    return lax.dot_general(image, text, (((1,), (1,)), ((), ())), preferred_element_type=F32)
+
+
+def head_kernel(parts_ref, grads_ref, out_ref):
+    sources, blocks, height, count = parts_ref.shape
+    cols = out_ref.shape[2]
+    total = jnp.zeros((blocks * height, cols), F32)
+    for s in range(sources):
+        total += score(parts_ref[s].reshape(blocks * height, count), grads_ref[pl.ds(s * cols, cols)])
+    out_ref[...] = total.astype(BF).reshape(out_ref.shape)
+
+
 def join_kernel(own_ref, other_ref, out_ref):
     blocks, height, _ = out_ref.shape
     cols = height - 16
@@ -143,13 +156,25 @@
     ).astype(BF)
     grad_pooled = lax.psum_scatter(grad_pooled, "x", scatter_dimension=0, tiled=True)
     given = jnp.where(yh == 0, grad_pooled[rows:], grad_pooled[:rows])
+    kept = jnp.where(yh == 0, grad_pooled[:rows], grad_pooled[rows:])
+    given, kept = lax.optimization_barrier((given, kept))
     taken = lax.ppermute(given, "yh", CORES)
-    kept = jnp.where(yh == 0, grad_pooled[:rows], grad_pooled[rows:])
     grad_pooled = kept.astype(F32) + taken.astype(F32)
 
-    grad_all = lax.all_gather(grad_proj, ("yl", "c"), axis=0)
-    grad_head = jnp.einsum("szri,sfi->zrf", parts, grad_all, preferred_element_type=F32).astype(BF)
+    grad_all = lax.all_gather(grad_proj, ("yl", "c"), axis=0, tiled=True)
+    grad_head = pl.pallas_call(
+        head_kernel,
+        out_shape=jax.ShapeDtypeStruct((NZ, padded, cols), BF),
+        compiler_params=pltpu.CompilerParams(vmem_limit_bytes=40 * 2**20),
+        cost_estimate=pl.CostEstimate(
+            flops=2 * NZ * padded * cols * count * NYL * NC,
+            bytes_accessed=2 * (parts.size + grad_all.size + NZ * padded * cols),
+            transcendentals=0,
+        ),
+        name="head_product",
+    )(parts, grad_all)
     grad_head = lax.all_to_all(grad_head, "z", split_axis=0, concat_axis=0, tiled=True)
+    grad_head, grad_pooled = lax.optimization_barrier((grad_head, grad_pooled))
     grad_head = jnp.sum(grad_head.astype(F32), axis=0)[:small]
     return (grad_pooled, grad_head)
 

time: 180 us -> 176 us (0.978); the launches traced: 177 us -> 175 us
  waiting for transfers between devices: 30.7 us -> 35.8 us
  local copies, waits for them, and re-layouts: 13.3 us -> 9.94 us
  matrix products: 4.24 us -> 1.82 us
  starting transfers between devices: 20.9 us -> 18.7 us
  Pallas kernels: 7.68 us -> 9.51 us
    ppermute x1, waiting for transfers between devices: 0.01 us -> 4.81 us  [per_device(): taken = lax.ppermute(given, 'yh', CORES)]
    all_to_all x1, waiting for transfers between devices: 4.68 us -> 0.01 us  [per_device(): lax.all_to_all(grad_head, 'z', split_axis=0, concat_axis=0, tiled=True)]
    all_gather x1, waiting for transfers between devices: 4.8 us -> 8.88 us  [per_device(): text_own = lax.all_gather(text_pair, 'z', axis=0, tiled=True)]
    unnamed x13 -> x4, local copies, waits for them, and re-layouts: 4.58 us -> 2.05 us
    dot_general x1 -> x0, matrix products: 2.4 us -> none  [per_device(): jnp.einsum('szri,sfi->zrf', parts, grad_all, preferred_element_type=F32)]
  transfers between devices with their start and end apart: 7 -> 7, of which waited for: 4 -> 4; matrix products, arithmetic and copies ran while one was open for 9% -> 7% of each run, Pallas kernels for 2% -> 2%
where the time goes in v5:
time: 176 us; the launch traced here: 175 us
  blocking collectives  78.7 us (45%)
  waiting for transfers between devices  35.8 us (20%)
  starting transfers between devices  18.7 us (11%)
  between operations  15.5 us (9%)
  local copies, waits for them, and re-layouts  9.94 us (6%)
  Pallas kernels  9.51 us (5%)
  other arithmetic  4.68 us (3%)
  matrix products  1.82 us (1%)
    all_gather x2, blocking collectives, gather_t(): lax.all_gather(lax.all_gather(v, 'yh', axis=0, tiled=True), 'x', axis=0,...  28.1 us
    all_to_all x1, blocking collectives, per_device(): block = lax.all_to_all(block, T, split_axis=0, concat_axis=0, tiled=True)  21.3 us
    all_gather x2, blocking collectives, gather_t(): lax.all_gather(v, 'yh', axis=0, tiled=True)  16.6 us
    all_to_all x1, waiting for transfers between devices, per_device(): lax.all_to_all(parts, ('yl', 'c'), split_axis=0, concat_axis=0, tiled=True)  11.3 us
    reduce_scatter x1, waiting for transfers between devices, per_device(): lax.psum_scatter(grad_pooled, 'x', scatter_dimension=0, tiled=True)  10.8 us
    all_gather x1, waiting for transfers between devices, per_device(): text_own = lax.all_gather(text_pair, 'z', axis=0, tiled=True)  8.88 us
    all_to_all x1, starting transfers between devices, per_device(): lax.all_to_all(grad_head, 'z', split_axis=0, concat_axis=0, tiled=True)  7.81 us
    pallas_call x2, Pallas kernels, pairs(): pl.pallas_call(lambda *refs: pairs_kernel(own, rows, *refs), in_specs=[sm...  6.44 us
  transfers between devices with their start and end apart: 7, of which 4 were waited for; matrix products, arithmetic and copies ran while one was open for 7% of the time, Pallas kernels for 2%

profile of v5, /device:TPU:24, one launch (start us, length us, event | category | flops | bytes accessed | tf_op | source)
XLA Modules:
  0.0 174.8 jit_solution(2159061101722465749)
XLA Ops:
  7.2 1.7 unit_texts.1
  9.0 6.4 %all_gather.21 = bf16[64,1792]{1,0:T(8,128)(2,1)} all-gather(bf16[32,1792]{1,0:T(8,128)(2,1)} %unit_texts.1), channel_id=1, replica_groups=mesh['z'=16,'yl'=2,'c'=2,'yh'=2,'x'=4] {'yl'}, dimensions={0}, use_global_device_ids=true | all-gather | bytes 344064 | tf_op jit(solution)/shard_map/all_gather | solution.py:114
  15.4 9.6 %all_gather.23 = bf16[64,1792]{1,0:T(8,128)(2,1)S(1)} all-gather(bf16[32,1792]{1,0:T(8,128)(2,1)} %param.5), channel_id=1, replica_groups=mesh['z'=16,'yl'=2,'c'=2,'yh'=2,'x'=4] {'yh'}, dimensions={0}, use_global_device_ids=true | all-gather | bytes 344064 | tf_op jit(solution)/shard_map/all_gather | solution.py:22
  25.0 14.6 %all_gather.24 = bf16[256,1792]{1,0:T(8,128)(2,1)S(1)} all-gather(bf16[64,1792]{1,0:T(8,128)(2,1)S(1)} %all_gather.23), channel_id=1, replica_groups=mesh['z'=16,'yl'=2,'c'=2,'yh'=2,'x'=4] {'x'}, dimensions={0}, use_global_device_ids=true | all-gather | bytes 1146880 | tf_op jit(solution)/shard_map/all_gather | solution.py:22
  39.6 0.4 convolution_convert_fusion.1
  40.0 7.0 %all_gather.25 = bf16[448,256]{1,0:T(8,128)(2,1)S(1)} all-gather(bf16[224,256]{1,0:T(8,128)(2,1)S(1)} %convolution_convert_fusion.1), channel_id=1, replica_groups=mesh['z'=16,'yl'=2,'c'=2,'yh'=2,'x'=4] {'yh'}, dimensions={0}, use_global_device_ids=true | all-gather | bytes 344064 | tf_op jit(solution)/shard_map/all_gather | solution.py:22
  47.0 13.6 %all_gather.26 = bf16[1792,256]{1,0:T(8,128)(2,1)S(1)} all-gather(bf16[448,256]{1,0:T(8,128)(2,1)S(1)} %all_gather.25), channel_id=1, replica_groups=mesh['z'=16,'yl'=2,'c'=2,'yh'=2,'x'=4] {'x'}, dimensions={0}, use_global_device_ids=true | all-gather | bytes 1146880 | tf_op jit(solution)/shard_map/all_gather | solution.py:22
  60.5 1.4 copy.8
  62.0 2.8 %copy.9 = f32[1792,256]{0,1:T(8,128)} copy(f32[1792,256]{1,0:T(8,128)} %bitcast.24) | data formatting | bytes 3670016 | tf_op jit(solution)/shard_map/convert_element_type | solution.py:16
  65.0 1.7 fusion.refs_3_
  66.7 1.9 %collective-permute-start = (bf16[256,1792]{1,0:T(8,128)(2,1)S(1)}, bf16[256,1792]{1,0:T(8,128)(2,1)}, u32[]{:S(2)}, u32[]{:S(2)}) collective-permute-start(bf16[256,1792]{1,0:T(8,128)(2,1)S(1)} %fusion.refs_3_), channel_id=1, source_target_pairs={{0,8},{8,0},{1,9},{9,1},{2,10},{10,2},{3,11},{11,3},{4,12},{12,4},... | collective-permute-start | bytes 2752520 | tf_op jit(solution)/shard_map/ppermute | solution.py:126
  68.6 1.3 copy.10
  69.9 1.3 reshape.32
  71.3 1.1 pad.4
  72.4 3.7 %all-to-all-start = ((bf16[4,16,32,256]{3,2,1,0:T(8,128)(2,1)}), bf16[4,16,32,256]{3,2,1,0:T(8,128)(2,1)S(1)}, u32[]{:S(2)}, u32[]{:S(2)}) async-start(bf16[4,16,32,256]{3,2,1,0:T(8,128)(2,1)} %pad.4), calls=%async_computation | async-start | bytes 2097152 | tf_op jit(solution)/shard_map/all_to_all | solution.py:132
  77.5 11.3 %all-to-all-done.parts_ref = bf16[4,16,32,256]{3,2,1,0:T(8,128)(2,1)S(1)} async-done(((bf16[4,16,32,256]{3,2,1,0:T(8,128)(2,1)}), bf16[4,16,32,256]{3,2,1,0:T(8,128)(2,1)S(1)}, u32[]{:S(2)}, u32[]{:S(2)}) %all-to-all-start) | async-done | bytes 1048608 | tf_op jit(solution)/shard_map/all_to_all | solution.py:132
  88.8 8.9 %all-gather.2.cloned.1.call-done.refs_2_ = bf16[1024,1792]{1,0:T(8,128)(2,1)} async-done(((bf16[64,1792]{1,0:T(8,128)(2,1)}), bf16[1024,1792]{1,0:T(8,128)(2,1)}) %all-gather.2.cloned.1.call-update) | async-done | bytes 3670032 | tf_op jit(solution)/shard_map/all_gather | solution.py:115
  97.7 2.0 %copy-done.1 = bf16[1024,1792]{1,0:T(8,128)(2,1)S(1)} copy-done((bf16[1024,1792]{1,0:T(8,128)(2,1)S(1)}, bf16[1024,1792]{1,0:T(8,128)(2,1)}, u32[]{:S(2)}) %copy-start.1) | copy-done | bytes 3670040
  99.7 3.5 %pairs_other.1 = bf16[1808,256]{1,0:T(8,128)(2,1)S(1)} custom-call(f32[2]{0:T(128)S(1)} %pad_maximum_fusion.refs_0_, s32[2]{0:T(128)S(1)} %pad_add_fusion.refs_1_, bf16[1024,1792]{1,0:T(8,128)(2,1)S(1)} %copy-done.1, bf16[256,1792]{1,0:T(8,128)(2,1)} %collective-permute-done.refs_3_), custom_call_target="tpu_custom_call" | custom-call | flops 1879048192 | bytes 5505024 | tf_op jit(solution)/shard_map/pairs_other/pallas_call | solution.py:61
  103.3 1.9 %collective-permute-start.1 = (bf16[1808,256]{1,0:T(8,128)(2,1)S(1)}, bf16[1808,256]{1,0:T(8,128)(2,1)S(1)}, u32[]{:S(2)}, u32[]{:S(2)}) collective-permute-start(bf16[1808,256]{1,0:T(8,128)(2,1)S(1)} %pairs_other.1), channel_id=1, source_target_pairs={{0,8},{8,0},{1,9},{9,1},{2,10},{10,2},{3,11},{11,3},{4,12},{12,4},... | collective-permute-start | bytes 2777096 | tf_op jit(solution)/shard_map/ppermute | solution.py:140
  105.2 2.9 %pairs_own.1.own_ref = f32[1808,256]{1,0:T(8,128)S(1)} custom-call(f32[2]{0:T(128)S(1)} %pad_maximum_fusion.refs_0_, s32[2]{0:T(128)S(1)} %pad_add_fusion.refs_1_, bf16[1024,1792]{1,0:T(8,128)(2,1)S(1)} %copy-done.1, bf16[256,1792]{1,0:T(8,128)(2,1)S(1)} %fusion.refs_3_), custom_call_target="tpu_custom_call" | custom-call | flops 1879048192 | bytes 5505024 | tf_op jit(solution)/shard_map/pairs_own/pallas_call | solution.py:61
  108.3 21.3 %all_to_all.15 = bf16[8,240,256]{2,1,0:T(8,128)(2,1)S(1)} all-to-all(bf16[8,240,256]{2,1,0:T(8,128)(2,1)S(1)} %join_cores.1), channel_id=1, replica_groups=mesh['z'=16,'yl'=2,'c'=2,'yh'=2,'x'=4] {'yh','x'}, dimensions={0} | all-to-all | bytes 1966080 | tf_op jit(solution)/shard_map/all_to_all | solution.py:148
  129.8 1.4 convolution_convert_fusion
  131.2 6.3 %all_gather.27.grads_ref = bf16[896,256]{1,0:T(8,128)(2,1)S(1)} all-gather(bf16[224,256]{1,0:T(8,128)(2,1)S(1)} %fusion.2), channel_id=1, replica_groups=mesh['z'=16,'yl'=2,'c'=2,'yh'=2,'x'=4] {'yl','c'}, dimensions={0}, use_global_device_ids=true | all-gather | bytes 573440 | tf_op jit(solution)/shard_map/all_gather | solution.py:164
  137.6 1.2 head_product.1
  138.8 7.8 %all-to-all-start.2 = ((bf16[16,32,224]{2,1,0:T(8,128)(2,1)}), bf16[16,32,224]{2,1,0:T(8,128)(2,1)S(1)}, u32[]{:S(2)}, u32[]{:S(2)}) async-start(bf16[16,32,224]{2,1,0:T(8,128)(2,1)} %head_product.1), calls=%async_computation.2 | async-start | bytes 524288 | tf_op jit(solution)/shard_map/all_to_all | solution.py:176
  146.6 10.8 %reduce-scatter.2.cloned.1.call-done = bf16[64,1792]{1,0:T(8,128)(2,1)} async-done(((bf16[256,1792]{1,0:T(8,128)(2,1)}), bf16[64,1792]{1,0:T(8,128)(2,1)}) %reduce-scatter.2.cloned.1.call-update) | async-done | bytes 229392 | tf_op jit(solution)/shard_map/reduce_scatter | solution.py:157
  157.4 1.0 broadcast_select_fusion
  158.3 3.4 %collective-permute-start.2 = (bf16[32,1792]{1,0:T(8,128)(2,1)S(1)}, bf16[32,1792]{1,0:T(8,128)(2,1)S(1)}, u32[]{:S(2)}, u32[]{:S(2)}) collective-permute-start(bf16[32,1792]{1,0:T(8,128)(2,1)S(1)} %get-tuple-element.17), channel_id=1, source_target_pairs={{0,4},{4,0},{1,5},{5,1},{2,6},{6,2},{3,7},{7,3},{8,12},{12,8},{9,1... | collective-permute-start | bytes 344072 | tf_op jit(solution)/shard_map/ppermute | solution.py:161
  161.7 4.8 %collective-permute-done.2 = bf16[32,1792]{1,0:T(8,128)(2,1)S(1)} collective-permute-done((bf16[32,1792]{1,0:T(8,128)(2,1)S(1)}, bf16[32,1792]{1,0:T(8,128)(2,1)S(1)}, u32[]{:S(2)}, u32[]{:S(2)}) %collective-permute-start.2) | collective-permute-done | bytes 114720 | tf_op jit(solution)/shard_map/ppermute | solution.py:161
  166.5 0.7 convert_add_fusion
  167.3 0.7 convert_reduce_fusion.1
  (20 shorter events, 1.0 us)
Async XLA Ops:
  7.2 32.4 %copy-start = (bf16[224,1792]{1,0:T(8,128)(2,1)S(1)}, bf16[224,1792]{1,0:T(8,128)(2,1)}, u32[]{:S(2)}) copy-start(bf16[224,1792]{1,0:T(8,128)(2,1)} %param.7) | copy-start | bytes 2408452
  7.2 90.5 %all-gather.2.cloned.1.call-start = ((), (), s32[]{:S(2)}) async-start(), calls=%async_computation.4 | async-start | bytes 3899392 | tf_op jit(solution)/shard_map/all_gather | solution.py:115
  66.7 22.1 %collective-permute-start = (bf16[256,1792]{1,0:T(8,128)(2,1)S(1)}, bf16[256,1792]{1,0:T(8,128)(2,1)}, u32[]{:S(2)}, u32[]{:S(2)}) collective-permute-start(bf16[256,1792]{1,0:T(8,128)(2,1)S(1)} %fusion.refs_3_), channel_id=1, source_target_pairs={{0,8},{8,0},{1,9},{9,1},{2,10},{10,2},{3,11},{11,3},{4,12},{12,4},... | collective-permute-start | bytes 2752520 | tf_op jit(solution)/shard_map/ppermute | solution.py:126
  72.4 16.5 %all-to-all-start = ((bf16[4,16,32,256]{3,2,1,0:T(8,128)(2,1)}), bf16[4,16,32,256]{3,2,1,0:T(8,128)(2,1)S(1)}, u32[]{:S(2)}, u32[]{:S(2)}) async-start(bf16[4,16,32,256]{3,2,1,0:T(8,128)(2,1)} %pad.4), calls=%async_computation | async-start | bytes 2097152 | tf_op jit(solution)/shard_map/all_to_all | solution.py:132
  76.0 81.4 %reduce-scatter.2.cloned.1.call-start = ((), (), s32[]{:S(2)}) async-start(), calls=%async_computation.5 | async-start | bytes 1146880 | tf_op jit(solution)/shard_map/reduce_scatter | solution.py:157
  97.7 2.0 %copy-start.1 = (bf16[1024,1792]{1,0:T(8,128)(2,1)S(1)}, bf16[1024,1792]{1,0:T(8,128)(2,1)}, u32[]{:S(2)}) copy-start(bf16[1024,1792]{1,0:T(8,128)(2,1)} %all-gather.2.cloned.1.call-done.refs_2_) | copy-start | bytes 11010052
  103.3 4.9 %collective-permute-start.1 = (bf16[1808,256]{1,0:T(8,128)(2,1)S(1)}, bf16[1808,256]{1,0:T(8,128)(2,1)S(1)}, u32[]{:S(2)}, u32[]{:S(2)}) collective-permute-start(bf16[1808,256]{1,0:T(8,128)(2,1)S(1)} %pairs_other.1), channel_id=1, source_target_pairs={{0,8},{8,0},{1,9},{9,1},{2,10},{10,2},{3,11},{11,3},{4,12},{12,4},... | collective-permute-start | bytes 2777096 | tf_op jit(solution)/shard_map/ppermute | solution.py:140
  138.8 28.5 %all-to-all-start.2 = ((bf16[16,32,224]{2,1,0:T(8,128)(2,1)}), bf16[16,32,224]{2,1,0:T(8,128)(2,1)S(1)}, u32[]{:S(2)}, u32[]{:S(2)}) async-start(bf16[16,32,224]{2,1,0:T(8,128)(2,1)} %head_product.1), calls=%async_computation.2 | async-start | bytes 524288 | tf_op jit(solution)/shard_map/all_to_all | solution.py:176
  158.3 8.2 %collective-permute-start.2 = (bf16[32,1792]{1,0:T(8,128)(2,1)S(1)}, bf16[32,1792]{1,0:T(8,128)(2,1)S(1)}, u32[]{:S(2)}, u32[]{:S(2)}) collective-permute-start(bf16[32,1792]{1,0:T(8,128)(2,1)S(1)} %get-tuple-element.17), channel_id=1, source_target_pairs={{0,4},{4,0},{1,5},{5,1},{2,6},{6,2},{3,7},{7,3},{8,12},{12,8},{9,1... | collective-permute-start | bytes 344072 | tf_op jit(solution)/shard_map/ppermute | solution.py:161
Sparse Core Ops, SparseCore 0:
  15.5 82.1 all-gather.1
  131.4 25.9 reduce-scatter.1

commit v6 on v5

v6 whole, which is shorter than its diff:
```python
import jax
import jax.numpy as jnp
from jax import lax
from jax.experimental import pallas as pl
from jax.experimental.pallas import tpu as pltpu
from jax.sharding import Mesh, PartitionSpec as P

BF = jnp.bfloat16
F32 = jnp.float32
T = ("yh", "x")
NZ, NYL, NC, NYH, NX = 16, 2, 2, 2, 4
CORES = [(0, 1), (1, 0)]


def unit(v, axis):
    v = v.astype(F32)
    norms = jnp.sqrt(jnp.sum(v * v, axis=axis, keepdims=True) + 1e-06)
    return v / norms, norms


def gather_t(v):
    return lax.all_gather(lax.all_gather(v, "yh", axis=0, tiled=True), "x", axis=0, tiled=True)


def unit_kernel(rows_ref, out_ref):
    v = rows_ref[...].astype(F32)
    out_ref[...] = (v / jnp.sqrt(jnp.sum(v * v, axis=1, keepdims=True) + 1e-06)).astype(BF)


def score(image, text):
    return lax.dot_general(image, text, (((1,), (1,)), ((), ())), preferred_element_type=F32)


def head_kernel(parts_ref, grads_ref, out_ref):
    sources, blocks, height, count = parts_ref.shape
    cols = grads_ref.shape[0] // sources
    total = jnp.zeros((blocks * height, cols), F32)
    for s in range(sources):
        total += score(parts_ref[s].reshape(blocks * height, count), grads_ref[pl.ds(s * cols, cols)])
    total = total.reshape(blocks, height, cols)[:, : out_ref.shape[1] // 2]
    rest = jnp.concatenate(
        [total[:, :, 128:], jnp.zeros((*total.shape[:2], 256 - cols), F32)], axis=2
    )
    out_ref[...] = jnp.concatenate([total[:, :, :128], rest], axis=1).astype(BF)


def pairs_kernel(rows, par_ref, pos_ref, text_hbm, image_hbm, out_ref, text_ref, image_ref, sems):
    chunks = sems.shape[0] - 1
    step = text_ref.shape[0] // chunks
    copies = [
        pltpu.make_async_copy(
            text_hbm.at[pl.ds(k * step, step)], text_ref.at[pl.ds(k * step, step)], sems.at[k]
        )
        for k in range(chunks)
    ]
    image_copy = pltpu.make_async_copy(image_hbm, image_ref, sems.at[chunks])
    image_copy.start()
    for copy in copies:
        copy.start()
    image_copy.wait()
    image = image_ref[...]
    terms = dots = None
    for k, copy in enumerate(copies):
        copy.wait()
        text = text_ref[pl.ds(k * step, step)]
        scores = score(image, text)
        logits = par_ref[0] * scores + par_ref[1]
        a = lax.broadcasted_iota(jnp.int32, scores.shape, 1) + (k * step - pos_ref[0])
        b = lax.broadcasted_iota(jnp.int32, scores.shape, 0) - pos_ref[1]
        sign = jnp.where((a == b) & (a >= 0) & (a < rows), -1.0, 1.0)
        pair = (sign / (1.0 + jnp.exp(-sign * logits))).astype(BF)
        dot = jnp.sum(pair.astype(F32) * scores, axis=1, keepdims=True)
        term = jnp.dot(pair, text, preferred_element_type=F32)
        terms = term if k == 0 else terms + term
        dots = dot if k == 0 else dots + dot
    blocks, height, count = out_ref.shape
    cols = height - 16
    lane = lax.broadcasted_iota(jnp.int32, (count, 128), 1)
    high = dots.astype(BF).astype(F32)
    tail = jnp.where(lane == 0, high, jnp.where(lane == 1, dots - high, 0.0)).T[:16].astype(BF)
    terms = terms.T.astype(BF)
    for t in range(blocks):
        out_ref[t, :cols] = terms[t * cols : (t + 1) * cols]
        out_ref[t, cols:] = tail


def pairs(rows, blocks, par, pos, text, image):
    count, width = image.shape
    smem = pl.BlockSpec(memory_space=pltpu.SMEM)
    hbm = pl.BlockSpec(memory_space=pl.ANY)
    return pl.pallas_call(
        lambda *refs: pairs_kernel(rows, *refs),
        in_specs=[smem, smem, hbm, hbm],
        out_specs=pl.BlockSpec(memory_space=pltpu.VMEM),
        out_shape=jax.ShapeDtypeStruct((blocks, width // blocks + 16, count), BF),
        scratch_shapes=[
            pltpu.VMEM(text.shape, BF),
            pltpu.VMEM(image.shape, BF),
            pltpu.SemaphoreType.DMA((3,)),
        ],
        compiler_params=pltpu.CompilerParams(vmem_limit_bytes=56 * 2**20),
        cost_estimate=pl.CostEstimate(
            flops=4 * count * width * text.shape[0],
            bytes_accessed=2 * width * (text.shape[0] + 2 * count),
            transcendentals=count * text.shape[0],
        ),
        name="pairs",
    )(par, pos, text, image)


def per_device(pooled, texts, head_w, log_scale, bias):
    z, yl, c = lax.axis_index("z"), lax.axis_index("yl"), lax.axis_index("c")
    yh, x = lax.axis_index("yh"), lax.axis_index("x")
    rows, width = pooled.shape
    cols = head_w.shape[0]
    scale = jnp.exp(log_scale[0])
    shift = bias[0]

    text_unit = pl.pallas_call(
        unit_kernel, out_shape=jax.ShapeDtypeStruct(texts.shape, BF), name="unit_texts"
    )(texts)
    text_pair = lax.all_gather(text_unit, "yl", axis=0, tiled=True)
    text_all = lax.all_gather(text_pair, ("c", "z"), axis=0, tiled=True)

    images = gather_t(pooled)
    count = images.shape[0]
    own_cols = lax.dot_general(
        head_w, images, (((1,), (1,)), ((), ())), preferred_element_type=F32
    ).astype(BF)
    proj = gather_t(own_cols).reshape(NX, NYH, cols, count)
    proj = proj.transpose(1, 0, 2, 3).reshape(width, count)
    unit_all, norms = unit(proj, 0)
    embedded = unit_all.astype(BF).T

    small = width // (NZ * NYL * NC)
    padded = -(-small // 16) * 16
    parts = images.T.reshape(NZ, NYL * NC, small, count).transpose(1, 0, 2, 3)
    parts = jnp.pad(parts, ((0, 0), (0, 0), (0, padded - small), (0, 0)))
    parts = lax.all_to_all(parts, ("yl", "c"), split_axis=0, concat_axis=0, tiled=True)

    text_all, embedded, norms, parts = lax.optimization_barrier(
        (text_all, embedded, norms, parts)
    )
    par = jnp.stack([scale, shift])
    pos = jnp.stack([((c * NZ + z) * NYL + yl) * rows, (x * NYH + yh) * rows]).astype(jnp.int32)
    block = pairs(rows, NYH * NX, par, pos, text_all, embedded)
    block = lax.all_to_all(block, T, split_axis=0, concat_axis=0, tiled=True)
    block = scale * jnp.sum(block.astype(F32), axis=0)
    row_dots = block[cols : cols + 1] + block[cols + 1 : cols + 2]
    own_unit = own_cols.astype(F32) / norms
    grad_proj = ((block[:cols] - own_unit * row_dots) / norms).astype(BF)

    grad_pooled = lax.dot_general(
        grad_proj, head_w, (((0,), (0,)), ((), ())), preferred_element_type=F32
    ).astype(BF)
    grad_pooled = lax.psum_scatter(grad_pooled, "x", scatter_dimension=0, tiled=True)
    given = jnp.where(yh == 0, grad_pooled[rows:], grad_pooled[:rows])
    kept = jnp.where(yh == 0, grad_pooled[:rows], grad_pooled[rows:])
    given, kept = lax.optimization_barrier((given, kept))
    taken = lax.ppermute(given, "yh", CORES)
    grad_pooled = kept.astype(F32) + taken.astype(F32)

    grad_all = lax.all_gather(grad_proj, ("yl", "c"), axis=0, tiled=True)
    grad_head = pl.pallas_call(
        head_kernel,
        out_shape=jax.ShapeDtypeStruct((NZ, 2 * small, 128), BF),
        compiler_params=pltpu.CompilerParams(vmem_limit_bytes=40 * 2**20),
        cost_estimate=pl.CostEstimate(
            flops=2 * NZ * padded * cols * count * NYL * NC,
            bytes_accessed=2 * (parts.size + grad_all.size + NZ * padded * cols),
            transcendentals=0,
        ),
        name="head_product",
    )(parts, grad_all)
    grad_head = lax.all_to_all(grad_head, "z", split_axis=0, concat_axis=0, tiled=True)
    grad_head, grad_pooled = lax.optimization_barrier((grad_head, grad_pooled))
    grad_head = jnp.sum(grad_head.astype(F32), axis=0)
    grad_head = jnp.concatenate(
        [grad_head[:small], grad_head[small:, : cols - 128]], axis=1
    )
    return (grad_pooled, grad_head)


def solution(mesh):
    fine = Mesh(mesh.devices.reshape(NZ, NYL, NC, NYH, NX), ("z", "yl", "c", "yh", "x"))
    dp = ("z", "yl", "c")
    rows = P(dp + T, None)
    return jax.shard_map(
        per_device,
        mesh=fine,
        in_specs=(rows, rows, P(T, None), P(), P()),
        out_specs=(rows, P(dp, T)),
        check_vma=False,
    )
```

time: 176 us -> 175 us (level)
  blocking collectives: 78.7 us -> 89 us
  waiting for transfers between devices: 35.8 us -> 25.8 us
  starting transfers between devices: 18.7 us -> 15 us
  Pallas kernels: 9.51 us -> 12.1 us
  other arithmetic: 4.68 us -> 6.67 us
    all_to_all x1, waiting for transfers between devices: 11.3 us -> 0.01 us  [per_device(): lax.all_to_all(parts, ('yl', 'c'), split_axis=0, concat_axis=0, tiled=True)]
    all_gather x2, blocking collectives: 16.6 us -> 25.9 us  [gather_t(): lax.all_gather(v, 'yh', axis=0, tiled=True)]
    ppermute x2 -> x0, starting transfers between devices: 3.84 us -> none  [the longest x1 1.92 us: per_device(): embedded_other = lax.ppermute(embedded, 'c', CORES)]
    pallas_call x4 -> x2, Pallas kernels: 7.77 us -> 10.3 us  [the longest x1 9.19 us: pairs(): pl.pallas_call(lambda *refs: pairs_kernel(rows, *refs), in_specs=[smem, s...]
    unnamed x4 -> x2, local copies, waits for them, and re-layouts: 2.05 us -> 0.01 us
  transfers between devices with their start and end apart: 7 -> 5, of which waited for: 4 -> 3; matrix products, arithmetic and copies ran while one was open for 7% -> 8% of each run, Pallas kernels for 2% -> 1%
where the time goes in v6:
time: 175 us; the launch traced here: 174 us
  blocking collectives  89 us (51%)
  waiting for transfers between devices  25.8 us (15%)
  between operations  15.5 us (9%)
  starting transfers between devices  15 us (9%)
  Pallas kernels  12.1 us (7%)
  local copies, waits for them, and re-layouts  8.34 us (5%)
  other arithmetic  6.67 us (4%)
  matrix products  1.82 us (1%)
    all_gather x2, blocking collectives, gather_t(): lax.all_gather(lax.all_gather(v, 'yh', axis=0, tiled=True), 'x', axis=0,...  29.3 us
    all_gather x2, blocking collectives, gather_t(): lax.all_gather(v, 'yh', axis=0, tiled=True)  25.9 us
    all_to_all x1, blocking collectives, per_device(): block = lax.all_to_all(block, T, split_axis=0, concat_axis=0, tiled=True)  21.1 us
    reduce_scatter x1, waiting for transfers between devices, per_device(): lax.psum_scatter(grad_pooled, 'x', scatter_dimension=0, tiled=True)  10.8 us
    all_gather x1, waiting for transfers between devices, per_device(): text_all = lax.all_gather(text_pair, ('c', 'z'), axis=0, tiled=True)  10.1 us
    pallas_call x1, Pallas kernels, pairs(): pl.pallas_call(lambda *refs: pairs_kernel(rows, *refs), in_specs=[smem, s...  9.19 us
    all_to_all x1, starting transfers between devices, per_device(): lax.all_to_all(grad_head, 'z', split_axis=0, concat_axis=0, tiled=True)  7.92 us
    all_gather x1, blocking collectives, per_device(): text_pair = lax.all_gather(text_unit, 'yl', axis=0, tiled=True)  6.38 us
  transfers between devices with their start and end apart: 5, of which 3 were waited for; matrix products, arithmetic and copies ran while one was open for 8% of the time, Pallas kernels for 1%

profile of v6, /device:TPU:24, one launch (start us, length us, event | category | flops | bytes accessed | tf_op | source)
XLA Modules:
  0.0 174.2 jit_solution(1768348436765589209)
XLA Ops:
  7.2 1.7 unit_texts.1
  9.0 6.4 %all_gather.21 = bf16[64,1792]{1,0:T(8,128)(2,1)} all-gather(bf16[32,1792]{1,0:T(8,128)(2,1)} %unit_texts.1), channel_id=1, replica_groups=mesh['z'=16,'yl'=2,'c'=2,'yh'=2,'x'=4] {'yl'}, dimensions={0}, use_global_device_ids=true | all-gather | bytes 344064 | tf_op jit(solution)/shard_map/all_gather | solution.py:122
  15.4 9.6 %all_gather.23 = bf16[64,1792]{1,0:T(8,128)(2,1)S(1)} all-gather(bf16[32,1792]{1,0:T(8,128)(2,1)} %param.5), channel_id=1, replica_groups=mesh['z'=16,'yl'=2,'c'=2,'yh'=2,'x'=4] {'yh'}, dimensions={0}, use_global_device_ids=true | all-gather | bytes 344064 | tf_op jit(solution)/shard_map/all_gather | solution.py:22
  25.0 14.6 %all_gather.24 = bf16[256,1792]{1,0:T(8,128)(2,1)S(1)} all-gather(bf16[64,1792]{1,0:T(8,128)(2,1)S(1)} %all_gather.23), channel_id=1, replica_groups=mesh['z'=16,'yl'=2,'c'=2,'yh'=2,'x'=4] {'x'}, dimensions={0}, use_global_device_ids=true | all-gather | bytes 1146880 | tf_op jit(solution)/shard_map/all_gather | solution.py:22
  39.6 0.5 copy.10
  40.1 1.2 reshape.32
  41.3 1.3 copy.13
  42.6 1.1 pad.4
  43.7 3.6 %all-to-all-start = ((bf16[4,16,32,256]{3,2,1,0:T(8,128)(2,1)}), bf16[4,16,32,256]{3,2,1,0:T(8,128)(2,1)S(1)}, u32[]{:S(2)}, u32[]{:S(2)}) async-start(bf16[4,16,32,256]{3,2,1,0:T(8,128)(2,1)} %pad.4), calls=%async_computation | async-start | bytes 2097152 | tf_op jit(solution)/shard_map/all_to_all | solution.py:139
  48.7 0.4 convolution_convert_fusion.1
  49.1 16.3 %all_gather.25 = bf16[448,256]{1,0:T(8,128)(2,1)S(1)} all-gather(bf16[224,256]{1,0:T(8,128)(2,1)S(1)} %convolution_convert_fusion.1), channel_id=1, replica_groups=mesh['z'=16,'yl'=2,'c'=2,'yh'=2,'x'=4] {'yh'}, dimensions={0}, use_global_device_ids=true | all-gather | bytes 344064 | tf_op jit(solution)/shard_map/all_gather | solution.py:22
  65.4 0.7 pad_add_fusion.refs_1_
  66.0 14.7 %all_gather.26 = bf16[1792,256]{1,0:T(8,128)(2,1)S(1)} all-gather(bf16[448,256]{1,0:T(8,128)(2,1)S(1)} %all_gather.25), channel_id=1, replica_groups=mesh['z'=16,'yl'=2,'c'=2,'yh'=2,'x'=4] {'x'}, dimensions={0}, use_global_device_ids=true | all-gather | bytes 1146880 | tf_op jit(solution)/shard_map/all_gather | solution.py:22
  80.8 0.3 multiply_reduce_fusion
  81.0 0.6 pad_maximum_fusion.1.refs_0_
  81.6 1.4 copy.8
  83.0 2.8 %copy.9 = f32[1792,256]{0,1:T(8,128)} copy(f32[1792,256]{1,0:T(8,128)} %bitcast.23) | data formatting | bytes 3670016 | tf_op jit(solution)/shard_map/convert_element_type | solution.py:16
  85.8 2.6 %fusion.refs_3_ = bf16[256,1792]{1,0:T(8,128)(2,1)} fusion(f32[1792,256]{0,1:T(8,128)} %copy.9, f32[256]{0:T(256)S(1)} %add_sqrt_fusion), kind=kLoop, calls=%fused_computation.6 | loop fusion | flops 917504 | bytes 2753536 | tf_op jit(solution)/shard_map/transpose | solution.py:133
  88.5 10.1 %all-gather.2.cloned.1.call-done.refs_2_ = bf16[2048,1792]{1,0:T(8,128)(2,1)} async-done(((bf16[64,1792]{1,0:T(8,128)(2,1)}), bf16[2048,1792]{1,0:T(8,128)(2,1)}) %all-gather.2.cloned.1.call-update) | async-done | bytes 7340048 | tf_op jit(solution)/shard_map/all_gather | solution.py:123
  98.6 9.2 %pairs.1 = bf16[8,240,256]{2,1,0:T(8,128)(2,1)} custom-call(f32[2]{0:T(128)} %pad_maximum_fusion.1.refs_0_, s32[2]{0:T(128)} %pad_add_fusion.refs_1_, bf16[2048,1792]{1,0:T(8,128)(2,1)} %all-gather.2.cloned.1.call-done.refs_2_, bf16[256,1792]{1,0:T(8,128)(2,1)} %fusion.refs_3_), custom_call_target="tpu_custom_call" | custom-call | flops 3758096384 | bytes 9175040 | tf_op jit(solution)/shard_map/pairs/pallas_call | solution.py:91
  107.8 21.1 %all_to_all.15 = bf16[8,240,256]{2,1,0:T(8,128)(2,1)S(1)} all-to-all(bf16[8,240,256]{2,1,0:T(8,128)(2,1)} %pairs.1), channel_id=1, replica_groups=mesh['z'=16,'yl'=2,'c'=2,'yh'=2,'x'=4] {'yh','x'}, dimensions={0} | all-to-all | bytes 1966080 | tf_op jit(solution)/shard_map/all_to_all | solution.py:147
  128.9 0.1 convert_reduce_fusion
  129.1 1.4 convolution_convert_fusion
  130.5 6.3 %all_gather.27.grads_ref = bf16[896,256]{1,0:T(8,128)(2,1)S(1)} all-gather(bf16[224,256]{1,0:T(8,128)(2,1)S(1)} %fusion.2), channel_id=1, replica_groups=mesh['z'=16,'yl'=2,'c'=2,'yh'=2,'x'=4] {'yl','c'}, dimensions={0}, use_global_device_ids=true | all-gather | bytes 573440 | tf_op jit(solution)/shard_map/all_gather | solution.py:163
  136.8 1.1 head_product.1
  138.0 7.9 %all-to-all-start.2 = ((bf16[16,56,128]{2,1,0:T(8,128)(2,1)}), bf16[16,56,128]{2,1,0:T(8,128)(2,1)S(1)}, u32[]{:S(2)}, u32[]{:S(2)}) async-start(bf16[16,56,128]{2,1,0:T(8,128)(2,1)} %head_product.1), calls=%async_computation.2 | async-start | bytes 458752 | tf_op jit(solution)/shard_map/all_to_all | solution.py:175
  145.9 10.8 %reduce-scatter.2.cloned.1.call-done = bf16[64,1792]{1,0:T(8,128)(2,1)} async-done(((bf16[256,1792]{1,0:T(8,128)(2,1)}), bf16[64,1792]{1,0:T(8,128)(2,1)}) %reduce-scatter.2.cloned.1.call-update) | async-done | bytes 229392 | tf_op jit(solution)/shard_map/reduce_scatter | solution.py:156
  156.7 1.0 broadcast_select_fusion
  157.7 3.4 %collective-permute-start = (bf16[32,1792]{1,0:T(8,128)(2,1)S(1)}, bf16[32,1792]{1,0:T(8,128)(2,1)S(1)}, u32[]{:S(2)}, u32[]{:S(2)}) collective-permute-start(bf16[32,1792]{1,0:T(8,128)(2,1)S(1)} %get-tuple-element.15), channel_id=1, source_target_pairs={{0,4},{4,0},{1,5},{5,1},{2,6},{6,2},{3,7},{7,3},{8,12},{12,8},{9,1... | collective-permute-start | bytes 344072 | tf_op jit(solution)/shard_map/ppermute | solution.py:160
  161.1 4.8 %collective-permute-done = bf16[32,1792]{1,0:T(8,128)(2,1)S(1)} collective-permute-done((bf16[32,1792]{1,0:T(8,128)(2,1)S(1)}, bf16[32,1792]{1,0:T(8,128)(2,1)S(1)}, u32[]{:S(2)}, u32[]{:S(2)}) %collective-permute-start) | collective-permute-done | bytes 114720 | tf_op jit(solution)/shard_map/ppermute | solution.py:160
  165.9 0.7 convert_add_fusion
  166.7 0.6 pad_maximum_fusion
  (15 shorter events, 0.2 us)
Async XLA Ops:
  7.2 41.5 %copy-start = (bf16[224,1792]{1,0:T(8,128)(2,1)S(1)}, bf16[224,1792]{1,0:T(8,128)(2,1)}, u32[]{:S(2)}) copy-start(bf16[224,1792]{1,0:T(8,128)(2,1)} %param.7) | copy-start | bytes 2408452
  7.2 91.4 %all-gather.2.cloned.1.call-start = ((), (), s32[]{:S(2)}) async-start(), calls=%async_computation.4 | async-start | bytes 7569408 | tf_op jit(solution)/shard_map/all_gather | solution.py:123
  43.7 44.8 %all-to-all-start = ((bf16[4,16,32,256]{3,2,1,0:T(8,128)(2,1)}), bf16[4,16,32,256]{3,2,1,0:T(8,128)(2,1)S(1)}, u32[]{:S(2)}, u32[]{:S(2)}) async-start(bf16[4,16,32,256]{3,2,1,0:T(8,128)(2,1)} %pad.4), calls=%async_computation | async-start | bytes 2097152 | tf_op jit(solution)/shard_map/all_to_all | solution.py:139
  47.3 109.4 %reduce-scatter.2.cloned.1.call-start = ((), (), s32[]{:S(2)}) async-start(), calls=%async_computation.5 | async-start | bytes 1146880 | tf_op jit(solution)/shard_map/reduce_scatter | solution.py:156
  138.0 28.6 %all-to-all-start.2 = ((bf16[16,56,128]{2,1,0:T(8,128)(2,1)}), bf16[16,56,128]{2,1,0:T(8,128)(2,1)S(1)}, u32[]{:S(2)}, u32[]{:S(2)}) async-start(bf16[16,56,128]{2,1,0:T(8,128)(2,1)} %head_product.1), calls=%async_computation.2 | async-start | bytes 458752 | tf_op jit(solution)/shard_map/all_to_all | solution.py:175
  157.7 8.2 %collective-permute-start = (bf16[32,1792]{1,0:T(8,128)(2,1)S(1)}, bf16[32,1792]{1,0:T(8,128)(2,1)S(1)}, u32[]{:S(2)}, u32[]{:S(2)}) collective-permute-start(bf16[32,1792]{1,0:T(8,128)(2,1)S(1)} %get-tuple-element.15), channel_id=1, source_target_pairs={{0,4},{4,0},{1,5},{5,1},{2,6},{6,2},{3,7},{7,3},{8,12},{12,8},{9,1... | collective-permute-start | bytes 344072 | tf_op jit(solution)/shard_map/ppermute | solution.py:160
Sparse Core Ops, SparseCore 0:
  15.5 83.0 all-gather.1
  130.6 26.0 reduce-scatter.1

commit v7 on v6

--- a/solution.py
+++ b/solution.py
@@ -45,42 +45,51 @@
 
 
 def pairs_kernel(rows, par_ref, pos_ref, text_hbm, image_hbm, out_ref, text_ref, image_ref, sems):
-    chunks = sems.shape[0] - 1
-    step = text_ref.shape[0] // chunks
+    blocks, height, count = out_ref.shape
+    cols = height - 16
+    total, width = text_ref.shape
+    parts = [(0, total // 4), (total // 4, total - total // 4)]
     copies = [
         pltpu.make_async_copy(
-            text_hbm.at[pl.ds(k * step, step)], text_ref.at[pl.ds(k * step, step)], sems.at[k]
+            text_hbm.at[pl.ds(at, size)], text_ref.at[pl.ds(at, size)], sems.at[k]
         )
-        for k in range(chunks)
+        for k, (at, size) in enumerate(parts)
     ]
-    image_copy = pltpu.make_async_copy(image_hbm, image_ref, sems.at[chunks])
+    image_copy = pltpu.make_async_copy(image_hbm, image_ref, sems.at[len(parts)])
     image_copy.start()
     for copy in copies:
         copy.start()
     image_copy.wait()
     image = image_ref[...]
-    terms = dots = None
-    for k, copy in enumerate(copies):
-        copy.wait()
-        text = text_ref[pl.ds(k * step, step)]
-        scores = score(image, text)
+
+    def pair_of(k):
+        at, size = parts[k]
+        copies[k].wait()
+        scores = score(image, text_ref[pl.ds(at, size)])
         logits = par_ref[0] * scores + par_ref[1]
-        a = lax.broadcasted_iota(jnp.int32, scores.shape, 1) + (k * step - pos_ref[0])
+        a = lax.broadcasted_iota(jnp.int32, scores.shape, 1) + (at - pos_ref[0])
         b = lax.broadcasted_iota(jnp.int32, scores.shape, 0) - pos_ref[1]
         sign = jnp.where((a == b) & (a >= 0) & (a < rows), -1.0, 1.0)
         pair = (sign / (1.0 + jnp.exp(-sign * logits))).astype(BF)
-        dot = jnp.sum(pair.astype(F32) * scores, axis=1, keepdims=True)
-        term = jnp.dot(pair, text, preferred_element_type=F32)
-        terms = term if k == 0 else terms + term
-        dots = dot if k == 0 else dots + dot
-    blocks, height, count = out_ref.shape
-    cols = height - 16
+        return pair, jnp.sum(pair.astype(F32) * scores, axis=1, keepdims=True)
+
+    pair, dots = pair_of(0)
+    terms = jnp.dot(pair, text_ref[pl.ds(*parts[0])], preferred_element_type=F32)
+    pair, dots_rest = pair_of(1)
+    dots += dots_rest
+    for at in range(0, width, 256):
+        term = jnp.dot(pair, text_ref[pl.ds(*parts[1]), pl.ds(at, 256)], preferred_element_type=F32)
+        term = (term + terms[:, at : at + 256]).T.astype(BF)
+        row = at
+        while row < at + 256:
+            t = row // cols
+            end = min((t + 1) * cols, at + 256)
+            out_ref[t, row - t * cols : end - t * cols] = term[row - at : end - at]
+            row = end
     lane = lax.broadcasted_iota(jnp.int32, (count, 128), 1)
     high = dots.astype(BF).astype(F32)
     tail = jnp.where(lane == 0, high, jnp.where(lane == 1, dots - high, 0.0)).T[:16].astype(BF)
-    terms = terms.T.astype(BF)
     for t in range(blocks):
-        out_ref[t, :cols] = terms[t * cols : (t + 1) * cols]
         out_ref[t, cols:] = tail
 
 
@@ -98,7 +107,7 @@
             pltpu.VMEM(image.shape, BF),
             pltpu.SemaphoreType.DMA((3,)),
         ],
-        compiler_params=pltpu.CompilerParams(vmem_limit_bytes=56 * 2**20),
+        compiler_params=pltpu.CompilerParams(vmem_limit_bytes=52 * 2**20),
         cost_estimate=pl.CostEstimate(
             flops=4 * count * width * text.shape[0],
             bytes_accessed=2 * width * (text.shape[0] + 2 * count),

time: 175 us -> 173 us (0.989)
  other arithmetic: 6.67 us -> 4.67 us
  waiting for transfers between devices: 25.8 us -> 27.8 us
    all_gather x1, waiting for transfers between devices: 10.1 us -> 12 us  [per_device(): text_all = lax.all_gather(text_pair, ('c', 'z'), axis=0, tiled=True)]
  transfers between devices with their start and end apart: 5 -> 5, of which waited for: 3 -> 3; matrix products, arithmetic and copies ran while one was open for 8% -> 7% of each run, Pallas kernels for 1% -> 1%
where the time goes in v7:
time: 173 us; the launch traced here: 172 us
  blocking collectives  88.9 us (51%)
  waiting for transfers between devices  27.8 us (16%)
  between operations  15.5 us (9%)
  starting transfers between devices  14.9 us (9%)
  Pallas kernels  10.4 us (6%)
  local copies, waits for them, and re-layouts  8.36 us (5%)
  other arithmetic  4.67 us (3%)
  matrix products  1.82 us (1%)
    all_gather x2, blocking collectives, gather_t(): lax.all_gather(lax.all_gather(v, 'yh', axis=0, tiled=True), 'x', axis=0,...  29.4 us
    all_gather x2, blocking collectives, gather_t(): lax.all_gather(v, 'yh', axis=0, tiled=True)  25.9 us
    all_to_all x1, blocking collectives, per_device(): block = lax.all_to_all(block, T, split_axis=0, concat_axis=0, tiled=True)  20.9 us
    all_gather x1, waiting for transfers between devices, per_device(): text_all = lax.all_gather(text_pair, ('c', 'z'), axis=0, tiled=True)  12 us
    reduce_scatter x1, waiting for transfers between devices, per_device(): lax.psum_scatter(grad_pooled, 'x', scatter_dimension=0, tiled=True)  10.9 us
    all_to_all x1, starting transfers between devices, per_device(): lax.all_to_all(grad_head, 'z', split_axis=0, concat_axis=0, tiled=True)  7.92 us
    pallas_call x1, Pallas kernels, pairs(): pl.pallas_call(lambda *refs: pairs_kernel(rows, *refs), in_specs=[smem, s...  7.54 us
    all_gather x1, blocking collectives, per_device(): text_pair = lax.all_gather(text_unit, 'yl', axis=0, tiled=True)  6.38 us
  transfers between devices with their start and end apart: 5, of which 3 were waited for; matrix products, arithmetic and copies ran while one was open for 7% of the time, Pallas kernels for 1%

profile of v7, /device:TPU:24, one launch (start us, length us, event | category | flops | bytes accessed | tf_op | source)
XLA Modules:
  0.0 172.3 jit_solution(1402358827776972224)
XLA Ops:
  7.2 1.7 %unit_texts.1 = bf16[32,1792]{1,0:T(8,128)(2,1)} custom-call(bf16[32,1792]{1,0:T(8,128)(2,1)} %rows_ref.1), custom_call_target="tpu_custom_call" | custom-call | tf_op jit(solution)/shard_map/unit_texts/pallas_call | solution.py:128
  9.0 6.4 %all_gather.21 = bf16[64,1792]{1,0:T(8,128)(2,1)} all-gather(bf16[32,1792]{1,0:T(8,128)(2,1)} %unit_texts.1), channel_id=1, replica_groups=mesh['z'=16,'yl'=2,'c'=2,'yh'=2,'x'=4] {'yl'}, dimensions={0}, use_global_device_ids=true | all-gather | bytes 344064 | tf_op jit(solution)/shard_map/all_gather | solution.py:131
  15.4 9.6 %all_gather.23 = bf16[64,1792]{1,0:T(8,128)(2,1)S(1)} all-gather(bf16[32,1792]{1,0:T(8,128)(2,1)} %param.5), channel_id=1, replica_groups=mesh['z'=16,'yl'=2,'c'=2,'yh'=2,'x'=4] {'yh'}, dimensions={0}, use_global_device_ids=true | all-gather | bytes 344064 | tf_op jit(solution)/shard_map/all_gather | solution.py:22
  25.0 14.6 %all_gather.24 = bf16[256,1792]{1,0:T(8,128)(2,1)S(1)} all-gather(bf16[64,1792]{1,0:T(8,128)(2,1)S(1)} %all_gather.23), channel_id=1, replica_groups=mesh['z'=16,'yl'=2,'c'=2,'yh'=2,'x'=4] {'x'}, dimensions={0}, use_global_device_ids=true | all-gather | bytes 1146880 | tf_op jit(solution)/shard_map/all_gather | solution.py:22
  39.6 0.5 copy.10
  40.1 1.2 reshape.32
  41.3 1.3 copy.13
  42.6 1.1 pad.4
  43.7 3.6 %all-to-all-start = ((bf16[4,16,32,256]{3,2,1,0:T(8,128)(2,1)}), bf16[4,16,32,256]{3,2,1,0:T(8,128)(2,1)S(1)}, u32[]{:S(2)}, u32[]{:S(2)}) async-start(bf16[4,16,32,256]{3,2,1,0:T(8,128)(2,1)} %pad.4), calls=%async_computation | async-start | bytes 2097152 | tf_op jit(solution)/shard_map/all_to_all | solution.py:148
  48.7 0.4 convolution_convert_fusion.1
  49.1 16.3 %all_gather.25 = bf16[448,256]{1,0:T(8,128)(2,1)S(1)} all-gather(bf16[224,256]{1,0:T(8,128)(2,1)S(1)} %convolution_convert_fusion.1), channel_id=1, replica_groups=mesh['z'=16,'yl'=2,'c'=2,'yh'=2,'x'=4] {'yh'}, dimensions={0}, use_global_device_ids=true | all-gather | bytes 344064 | tf_op jit(solution)/shard_map/all_gather | solution.py:22
  65.4 0.1 pad_add_fusion.refs_1_
  65.4 14.8 %all_gather.26 = bf16[1792,256]{1,0:T(8,128)(2,1)S(1)} all-gather(bf16[448,256]{1,0:T(8,128)(2,1)S(1)} %all_gather.25), channel_id=1, replica_groups=mesh['z'=16,'yl'=2,'c'=2,'yh'=2,'x'=4] {'x'}, dimensions={0}, use_global_device_ids=true | all-gather | bytes 1146880 | tf_op jit(solution)/shard_map/all_gather | solution.py:22
  80.3 0.3 multiply_reduce_fusion
  80.5 0.1 pad_maximum_fusion.1.refs_0_
  80.6 1.5 copy.8
  82.1 2.8 %copy.9 = f32[1792,256]{0,1:T(8,128)} copy(f32[1792,256]{1,0:T(8,128)} %bitcast.23) | data formatting | bytes 3670016 | tf_op jit(solution)/shard_map/convert_element_type | solution.py:16
  84.9 1.7 fusion.refs_3_
  86.6 12.0 %all-gather.2.cloned.1.call-done.refs_2_ = bf16[2048,1792]{1,0:T(8,128)(2,1)} async-done(((bf16[64,1792]{1,0:T(8,128)(2,1)}), bf16[2048,1792]{1,0:T(8,128)(2,1)}) %all-gather.2.cloned.1.call-update) | async-done | bytes 7340048 | tf_op jit(solution)/shard_map/all_gather | solution.py:132
  98.6 7.5 %pairs.1 = bf16[8,240,256]{2,1,0:T(8,128)(2,1)S(1)} custom-call(f32[2]{0:T(128)S(1)} %pad_maximum_fusion.1.refs_0_, s32[2]{0:T(128)S(1)} %pad_add_fusion.refs_1_, bf16[2048,1792]{1,0:T(8,128)(2,1)} %all-gather.2.cloned.1.call-done.refs_2_, bf16[256,1792]{1,0:T(8,128)(2,1)S(1)} %fusion.refs_3_), custom_call_target="tpu_custom_call" | custom-call | flops 3758096384 | bytes 9175040 | tf_op jit(solution)/shard_map/pairs/pallas_call | solution.py:100
  106.1 20.9 %all_to_all.15 = bf16[8,240,256]{2,1,0:T(8,128)(2,1)S(1)} all-to-all(bf16[8,240,256]{2,1,0:T(8,128)(2,1)S(1)} %pairs.1), channel_id=1, replica_groups=mesh['z'=16,'yl'=2,'c'=2,'yh'=2,'x'=4] {'yh','x'}, dimensions={0} | all-to-all | bytes 1966080 | tf_op jit(solution)/shard_map/all_to_all | solution.py:156
  127.0 0.1 convert_reduce_fusion
  127.2 1.4 convolution_convert_fusion
  128.6 6.3 %all_gather.27.grads_ref = bf16[896,256]{1,0:T(8,128)(2,1)S(1)} all-gather(bf16[224,256]{1,0:T(8,128)(2,1)S(1)} %fusion.2), channel_id=1, replica_groups=mesh['z'=16,'yl'=2,'c'=2,'yh'=2,'x'=4] {'yl','c'}, dimensions={0}, use_global_device_ids=true | all-gather | bytes 573440 | tf_op jit(solution)/shard_map/all_gather | solution.py:172
  135.0 1.1 head_product.1
  136.1 7.9 %all-to-all-start.2 = ((bf16[16,56,128]{2,1,0:T(8,128)(2,1)}), bf16[16,56,128]{2,1,0:T(8,128)(2,1)S(1)}, u32[]{:S(2)}, u32[]{:S(2)}) async-start(bf16[16,56,128]{2,1,0:T(8,128)(2,1)} %head_product.1), calls=%async_computation.2 | async-start | bytes 458752 | tf_op jit(solution)/shard_map/all_to_all | solution.py:184
  144.1 10.9 %reduce-scatter.2.cloned.1.call-done = bf16[64,1792]{1,0:T(8,128)(2,1)} async-done(((bf16[256,1792]{1,0:T(8,128)(2,1)}), bf16[64,1792]{1,0:T(8,128)(2,1)}) %reduce-scatter.2.cloned.1.call-update) | async-done | bytes 229392 | tf_op jit(solution)/shard_map/reduce_scatter | solution.py:165
  154.9 1.0 broadcast_select_fusion
  155.9 3.3 %collective-permute-start = (bf16[32,1792]{1,0:T(8,128)(2,1)S(1)}, bf16[32,1792]{1,0:T(8,128)(2,1)S(1)}, u32[]{:S(2)}, u32[]{:S(2)}) collective-permute-start(bf16[32,1792]{1,0:T(8,128)(2,1)S(1)} %get-tuple-element.15), channel_id=1, source_target_pairs={{0,4},{4,0},{1,5},{5,1},{2,6},{6,2},{3,7},{7,3},{8,12},{12,8},{9,1... | collective-permute-start | bytes 344072 | tf_op jit(solution)/shard_map/ppermute | solution.py:169
  159.2 4.9 %collective-permute-done = bf16[32,1792]{1,0:T(8,128)(2,1)S(1)} collective-permute-done((bf16[32,1792]{1,0:T(8,128)(2,1)S(1)}, bf16[32,1792]{1,0:T(8,128)(2,1)S(1)}, u32[]{:S(2)}, u32[]{:S(2)}) %collective-permute-start) | collective-permute-done | bytes 114720 | tf_op jit(solution)/shard_map/ppermute | solution.py:169
  164.1 0.7 convert_add_fusion
  164.9 0.6 pad_maximum_fusion
  (15 shorter events, 0.2 us)
Async XLA Ops:
  7.2 41.5 %copy-start = (bf16[224,1792]{1,0:T(8,128)(2,1)S(1)}, bf16[224,1792]{1,0:T(8,128)(2,1)}, u32[]{:S(2)}) copy-start(bf16[224,1792]{1,0:T(8,128)(2,1)} %param.7) | copy-start | bytes 2408452
  7.2 91.4 %all-gather.2.cloned.1.call-start = ((), (), s32[]{:S(2)}) async-start(), calls=%async_computation.4 | async-start | bytes 7569408 | tf_op jit(solution)/shard_map/all_gather | solution.py:132
  43.7 42.9 %all-to-all-start = ((bf16[4,16,32,256]{3,2,1,0:T(8,128)(2,1)}), bf16[4,16,32,256]{3,2,1,0:T(8,128)(2,1)S(1)}, u32[]{:S(2)}, u32[]{:S(2)}) async-start(bf16[4,16,32,256]{3,2,1,0:T(8,128)(2,1)} %pad.4), calls=%async_computation | async-start | bytes 2097152 | tf_op jit(solution)/shard_map/all_to_all | solution.py:148
  47.3 107.6 %reduce-scatter.2.cloned.1.call-start = ((), (), s32[]{:S(2)}) async-start(), calls=%async_computation.5 | async-start | bytes 1146880 | tf_op jit(solution)/shard_map/reduce_scatter | solution.py:165
  136.1 28.7 %all-to-all-start.2 = ((bf16[16,56,128]{2,1,0:T(8,128)(2,1)}), bf16[16,56,128]{2,1,0:T(8,128)(2,1)S(1)}, u32[]{:S(2)}, u32[]{:S(2)}) async-start(bf16[16,56,128]{2,1,0:T(8,128)(2,1)} %head_product.1), calls=%async_computation.2 | async-start | bytes 458752 | tf_op jit(solution)/shard_map/all_to_all | solution.py:184
  155.9 8.2 %collective-permute-start = (bf16[32,1792]{1,0:T(8,128)(2,1)S(1)}, bf16[32,1792]{1,0:T(8,128)(2,1)S(1)}, u32[]{:S(2)}, u32[]{:S(2)}) collective-permute-start(bf16[32,1792]{1,0:T(8,128)(2,1)S(1)} %get-tuple-element.15), channel_id=1, source_target_pairs={{0,4},{4,0},{1,5},{5,1},{2,6},{6,2},{3,7},{7,3},{8,12},{12,8},{9,1... | collective-permute-start | bytes 344072 | tf_op jit(solution)/shard_map/ppermute | solution.py:169
Sparse Core Ops, SparseCore 0:
  15.5 83.0 all-gather.1
  128.8 26.1 reduce-scatter.1

commit v8 on v7

--- a/solution.py
+++ b/solution.py
@@ -44,9 +44,9 @@
     out_ref[...] = jnp.concatenate([total[:, :, :128], rest], axis=1).astype(BF)
 
 
-def pairs_kernel(rows, par_ref, pos_ref, text_hbm, image_hbm, out_ref, text_ref, image_ref, sems):
-    blocks, height, count = out_ref.shape
-    cols = height - 16
+def pairs_kernel(rows, par_ref, pos_ref, text_hbm, image_ref, out_ref, text_ref, sems):
+    blocks, height = out_ref.shape[0], out_ref.shape[1] // 2
+    count, cols = image_ref.shape[0], height - 16
     total, width = text_ref.shape
     parts = [(0, total // 4), (total // 4, total - total // 4)]
     copies = [
@@ -55,11 +55,8 @@
         )
         for k, (at, size) in enumerate(parts)
     ]
-    image_copy = pltpu.make_async_copy(image_hbm, image_ref, sems.at[len(parts)])
-    image_copy.start()
     for copy in copies:
         copy.start()
-    image_copy.wait()
     image = image_ref[...]
 
     def pair_of(k):
@@ -84,29 +81,29 @@
         while row < at + 256:
             t = row // cols
             end = min((t + 1) * cols, at + 256)
-            out_ref[t, row - t * cols : end - t * cols] = term[row - at : end - at]
+            for low in (0, 1):
+                out_ref[t, pl.ds(low * height + row - t * cols, end - row)] = term[
+                    row - at : end - at, low * 128 : low * 128 + 128
+                ]
             row = end
     lane = lax.broadcasted_iota(jnp.int32, (count, 128), 1)
     high = dots.astype(BF).astype(F32)
     tail = jnp.where(lane == 0, high, jnp.where(lane == 1, dots - high, 0.0)).T[:16].astype(BF)
     for t in range(blocks):
-        out_ref[t, cols:] = tail
+        for low in (0, 1):
+            out_ref[t, pl.ds(low * height + cols, 16)] = tail[:, low * 128 : low * 128 + 128]
 
 
 def pairs(rows, blocks, par, pos, text, image):
     count, width = image.shape
     smem = pl.BlockSpec(memory_space=pltpu.SMEM)
-    hbm = pl.BlockSpec(memory_space=pl.ANY)
+    vmem = pl.BlockSpec(memory_space=pltpu.VMEM)
     return pl.pallas_call(
         lambda *refs: pairs_kernel(rows, *refs),
-        in_specs=[smem, smem, hbm, hbm],
-        out_specs=pl.BlockSpec(memory_space=pltpu.VMEM),
-        out_shape=jax.ShapeDtypeStruct((blocks, width // blocks + 16, count), BF),
-        scratch_shapes=[
-            pltpu.VMEM(text.shape, BF),
-            pltpu.VMEM(image.shape, BF),
-            pltpu.SemaphoreType.DMA((3,)),
-        ],
+        in_specs=[smem, smem, pl.BlockSpec(memory_space=pl.ANY), vmem],
+        out_specs=vmem,
+        out_shape=jax.ShapeDtypeStruct((blocks, 2 * (width // blocks + 16), count // 2), BF),
+        scratch_shapes=[pltpu.VMEM(text.shape, BF), pltpu.SemaphoreType.DMA((2,))],
         compiler_params=pltpu.CompilerParams(vmem_limit_bytes=52 * 2**20),
         cost_estimate=pl.CostEstimate(
             flops=4 * count * width * text.shape[0],
@@ -147,17 +144,20 @@
     parts = jnp.pad(parts, ((0, 0), (0, 0), (0, padded - small), (0, 0)))
     parts = lax.all_to_all(parts, ("yl", "c"), split_axis=0, concat_axis=0, tiled=True)
 
-    text_all, embedded, norms, parts = lax.optimization_barrier(
-        (text_all, embedded, norms, parts)
+    norms = jnp.stack([norms[:, : count // 2], norms[:, count // 2 :]])
+    own_unit = jnp.stack([own_cols[:, : count // 2], own_cols[:, count // 2 :]])
+    own_unit = own_unit.astype(F32) / norms
+    text_all, embedded, norms, own_unit, parts = lax.optimization_barrier(
+        (text_all, embedded, norms, own_unit, parts)
     )
     par = jnp.stack([scale, shift])
     pos = jnp.stack([((c * NZ + z) * NYL + yl) * rows, (x * NYH + yh) * rows]).astype(jnp.int32)
     block = pairs(rows, NYH * NX, par, pos, text_all, embedded)
     block = lax.all_to_all(block, T, split_axis=0, concat_axis=0, tiled=True)
-    block = scale * jnp.sum(block.astype(F32), axis=0)
-    row_dots = block[cols : cols + 1] + block[cols + 1 : cols + 2]
-    own_unit = own_cols.astype(F32) / norms
-    grad_proj = ((block[:cols] - own_unit * row_dots) / norms).astype(BF)
+    block = scale * jnp.sum(block.astype(F32), axis=0).reshape(2, cols + 16, count // 2)
+    row_dots = block[:, cols : cols + 1] + block[:, cols + 1 : cols + 2]
+    grad_proj = ((block[:, :cols] - own_unit * row_dots) / norms).astype(BF)
+    grad_proj = jnp.concatenate([grad_proj[0], grad_proj[1]], axis=1)
 
     grad_pooled = lax.dot_general(
         grad_proj, head_w, (((0,), (0,)), ((), ())), preferred_element_type=F32

time: 173 us -> 173 us (level)
  no operation moved by 1% of the time
where the time goes in v8:
time: 173 us; the launch traced here: 172 us
  blocking collectives  89 us (51%)
  waiting for transfers between devices  27.5 us (16%)
  between operations  15.5 us (9%)
  starting transfers between devices  14.9 us (9%)
  Pallas kernels  10.2 us (6%)
  local copies, waits for them, and re-layouts  8.38 us (5%)
  other arithmetic  4.73 us (3%)
  matrix products  1.82 us (1%)
    all_gather x2, blocking collectives, gather_t(): lax.all_gather(lax.all_gather(v, 'yh', axis=0, tiled=True), 'x', axis=0,...  29.4 us
    all_gather x2, blocking collectives, gather_t(): lax.all_gather(v, 'yh', axis=0, tiled=True)  25.9 us
    all_to_all x1, blocking collectives, per_device(): block = lax.all_to_all(block, T, split_axis=0, concat_axis=0, tiled=True)  20.9 us
    all_gather x1, waiting for transfers between devices, per_device(): text_all = lax.all_gather(text_pair, ('c', 'z'), axis=0, tiled=True)  11.8 us
    reduce_scatter x1, waiting for transfers between devices, per_device(): lax.psum_scatter(grad_pooled, 'x', scatter_dimension=0, tiled=True)  10.8 us
    all_to_all x1, starting transfers between devices, per_device(): lax.all_to_all(grad_head, 'z', split_axis=0, concat_axis=0, tiled=True)  7.93 us
    pallas_call x1, Pallas kernels, pairs(): pl.pallas_call(lambda *refs: pairs_kernel(rows, *refs), in_specs=[smem, s...  7.31 us
    all_gather x1, blocking collectives, per_device(): text_pair = lax.all_gather(text_unit, 'yl', axis=0, tiled=True)  6.39 us
  transfers between devices with their start and end apart: 5, of which 3 were waited for; matrix products, arithmetic and copies ran while one was open for 7% of the time, Pallas kernels for 1%

profile of v8, /device:TPU:24, one launch (start us, length us, event | category | flops | bytes accessed | tf_op | source)
XLA Modules:
  0.0 172.1 jit_solution(7341353132591949765)
XLA Ops:
  7.2 1.7 %unit_texts.1 = bf16[32,1792]{1,0:T(8,128)(2,1)} custom-call(bf16[32,1792]{1,0:T(8,128)(2,1)} %rows_ref.1), custom_call_target="tpu_custom_call" | custom-call | tf_op jit(solution)/shard_map/unit_texts/pallas_call | solution.py:125
  9.0 6.4 %all_gather.21 = bf16[64,1792]{1,0:T(8,128)(2,1)} all-gather(bf16[32,1792]{1,0:T(8,128)(2,1)} %unit_texts.1), channel_id=1, replica_groups=mesh['z'=16,'yl'=2,'c'=2,'yh'=2,'x'=4] {'yl'}, dimensions={0}, use_global_device_ids=true | all-gather | bytes 344064 | tf_op jit(solution)/shard_map/all_gather | solution.py:128
  15.4 9.6 %all_gather.23 = bf16[64,1792]{1,0:T(8,128)(2,1)S(1)} all-gather(bf16[32,1792]{1,0:T(8,128)(2,1)} %param.5), channel_id=1, replica_groups=mesh['z'=16,'yl'=2,'c'=2,'yh'=2,'x'=4] {'yh'}, dimensions={0}, use_global_device_ids=true | all-gather | bytes 344064 | tf_op jit(solution)/shard_map/all_gather | solution.py:22
  25.0 14.6 %all_gather.24 = bf16[256,1792]{1,0:T(8,128)(2,1)S(1)} all-gather(bf16[64,1792]{1,0:T(8,128)(2,1)S(1)} %all_gather.23), channel_id=1, replica_groups=mesh['z'=16,'yl'=2,'c'=2,'yh'=2,'x'=4] {'x'}, dimensions={0}, use_global_device_ids=true | all-gather | bytes 1146880 | tf_op jit(solution)/shard_map/all_gather | solution.py:22
  39.6 0.5 copy.10
  40.1 1.2 reshape.35
  41.3 1.3 copy.13
  42.6 1.1 pad.4
  43.7 3.6 %all-to-all-start = ((bf16[4,16,32,256]{3,2,1,0:T(8,128)(2,1)}), bf16[4,16,32,256]{3,2,1,0:T(8,128)(2,1)S(1)}, u32[]{:S(2)}, u32[]{:S(2)}) async-start(bf16[4,16,32,256]{3,2,1,0:T(8,128)(2,1)} %pad.4), calls=%async_computation | async-start | bytes 2097152 | tf_op jit(solution)/shard_map/all_to_all | solution.py:145
  48.7 0.4 convolution_convert_fusion.1
  49.1 16.3 %all_gather.25 = bf16[448,256]{1,0:T(8,128)(2,1)S(1)} all-gather(bf16[224,256]{1,0:T(8,128)(2,1)S(1)} %convolution_convert_fusion.1), channel_id=1, replica_groups=mesh['z'=16,'yl'=2,'c'=2,'yh'=2,'x'=4] {'yh'}, dimensions={0}, use_global_device_ids=true | all-gather | bytes 344064 | tf_op jit(solution)/shard_map/all_gather | solution.py:22
  65.4 0.1 pad_add_fusion.refs_1_
  65.5 14.8 %all_gather.26 = bf16[1792,256]{1,0:T(8,128)(2,1)S(1)} all-gather(bf16[448,256]{1,0:T(8,128)(2,1)S(1)} %all_gather.25), channel_id=1, replica_groups=mesh['z'=16,'yl'=2,'c'=2,'yh'=2,'x'=4] {'x'}, dimensions={0}, use_global_device_ids=true | all-gather | bytes 1146880 | tf_op jit(solution)/shard_map/all_gather | solution.py:22
  80.3 0.3 multiply_reduce_fusion
  80.6 0.1 pad_maximum_fusion.3.refs_0_
  80.7 1.5 copy.8
  82.2 2.7 %copy.9 = f32[1792,256]{0,1:T(8,128)} copy(f32[1792,256]{1,0:T(8,128)} %bitcast.36) | data formatting | bytes 3670016 | tf_op jit(solution)/shard_map/convert_element_type | solution.py:16
  85.0 1.7 fusion.refs_3_
  86.7 11.8 %all-gather.2.cloned.1.call-done.refs_2_ = bf16[2048,1792]{1,0:T(8,128)(2,1)} async-done(((bf16[64,1792]{1,0:T(8,128)(2,1)}), bf16[2048,1792]{1,0:T(8,128)(2,1)}) %all-gather.2.cloned.1.call-update) | async-done | bytes 7340048 | tf_op jit(solution)/shard_map/all_gather | solution.py:129
  98.5 7.3 %pairs.1 = bf16[8,480,128]{2,1,0:T(8,128)(2,1)S(1)} custom-call(f32[2]{0:T(128)S(1)} %pad_maximum_fusion.3.refs_0_, s32[2]{0:T(128)S(1)} %pad_add_fusion.refs_1_, bf16[2048,1792]{1,0:T(8,128)(2,1)} %all-gather.2.cloned.1.call-done.refs_2_, bf16[256,1792]{1,0:T(8,128)(2,1)S(1)} %fusion.refs_3_), custom_call_target="tpu_custom_call" | custom-call | flops 3758096384 | bytes 9175040 | tf_op jit(solution)/shard_map/pairs/pallas_call | solution.py:101
  105.8 20.9 %all_to_all.15 = bf16[8,480,128]{2,1,0:T(8,128)(2,1)S(1)} all-to-all(bf16[8,480,128]{2,1,0:T(8,128)(2,1)S(1)} %pairs.1), channel_id=1, replica_groups=mesh['z'=16,'yl'=2,'c'=2,'yh'=2,'x'=4] {'yh','x'}, dimensions={0} | all-to-all | bytes 1966080 | tf_op jit(solution)/shard_map/all_to_all | solution.py:156
  126.8 0.1 convert_reduce_fusion
  127.0 1.4 convolution_convert_fusion
  128.5 6.3 %all_gather.27.grads_ref = bf16[896,256]{1,0:T(8,128)(2,1)S(1)} all-gather(bf16[224,256]{1,0:T(8,128)(2,1)S(1)} %pad_maximum_fusion), channel_id=1, replica_groups=mesh['z'=16,'yl'=2,'c'=2,'yh'=2,'x'=4] {'yl','c'}, dimensions={0}, use_global_device_ids=true | all-gather | bytes 573440 | tf_op jit(solution)/shard_map/all_gather | solution.py:172
  134.8 1.2 head_product.1
  136.0 7.9 %all-to-all-start.2 = ((bf16[16,56,128]{2,1,0:T(8,128)(2,1)}), bf16[16,56,128]{2,1,0:T(8,128)(2,1)S(1)}, u32[]{:S(2)}, u32[]{:S(2)}) async-start(bf16[16,56,128]{2,1,0:T(8,128)(2,1)} %head_product.1), calls=%async_computation.2 | async-start | bytes 458752 | tf_op jit(solution)/shard_map/all_to_all | solution.py:184
  143.9 10.8 %reduce-scatter.2.cloned.1.call-done = bf16[64,1792]{1,0:T(8,128)(2,1)} async-done(((bf16[256,1792]{1,0:T(8,128)(2,1)}), bf16[64,1792]{1,0:T(8,128)(2,1)}) %reduce-scatter.2.cloned.1.call-update) | async-done | bytes 229392 | tf_op jit(solution)/shard_map/reduce_scatter | solution.py:165
  154.7 1.0 broadcast_select_fusion
  155.7 3.3 %collective-permute-start = (bf16[32,1792]{1,0:T(8,128)(2,1)S(1)}, bf16[32,1792]{1,0:T(8,128)(2,1)S(1)}, u32[]{:S(2)}, u32[]{:S(2)}) collective-permute-start(bf16[32,1792]{1,0:T(8,128)(2,1)S(1)} %get-tuple-element.17), channel_id=1, source_target_pairs={{0,4},{4,0},{1,5},{5,1},{2,6},{6,2},{3,7},{7,3},{8,12},{12,8},{9,1... | collective-permute-start | bytes 344072 | tf_op jit(solution)/shard_map/ppermute | solution.py:169
  159.0 4.8 %collective-permute-done = bf16[32,1792]{1,0:T(8,128)(2,1)S(1)} collective-permute-done((bf16[32,1792]{1,0:T(8,128)(2,1)S(1)}, bf16[32,1792]{1,0:T(8,128)(2,1)S(1)}, u32[]{:S(2)}, u32[]{:S(2)}) %collective-permute-start) | collective-permute-done | bytes 114720 | tf_op jit(solution)/shard_map/ppermute | solution.py:169
  163.9 0.7 convert_add_fusion
  164.7 0.6 pad_maximum_fusion.1
  (21 shorter events, 0.3 us)
Async XLA Ops:
  7.2 41.5 %copy-start = (bf16[224,1792]{1,0:T(8,128)(2,1)S(1)}, bf16[224,1792]{1,0:T(8,128)(2,1)}, u32[]{:S(2)}) copy-start(bf16[224,1792]{1,0:T(8,128)(2,1)} %param.7) | copy-start | bytes 2408452
  7.2 91.3 %all-gather.2.cloned.1.call-start = ((), (), s32[]{:S(2)}) async-start(), calls=%async_computation.4 | async-start | bytes 7569408 | tf_op jit(solution)/shard_map/all_gather | solution.py:129
  43.7 43.0 %all-to-all-start = ((bf16[4,16,32,256]{3,2,1,0:T(8,128)(2,1)}), bf16[4,16,32,256]{3,2,1,0:T(8,128)(2,1)S(1)}, u32[]{:S(2)}, u32[]{:S(2)}) async-start(bf16[4,16,32,256]{3,2,1,0:T(8,128)(2,1)} %pad.4), calls=%async_computation | async-start | bytes 2097152 | tf_op jit(solution)/shard_map/all_to_all | solution.py:145
  47.3 107.4 %reduce-scatter.2.cloned.1.call-start = ((), (), s32[]{:S(2)}) async-start(), calls=%async_computation.5 | async-start | bytes 1146880 | tf_op jit(solution)/shard_map/reduce_scatter | solution.py:165
  136.0 28.6 %all-to-all-start.2 = ((bf16[16,56,128]{2,1,0:T(8,128)(2,1)}), bf16[16,56,128]{2,1,0:T(8,128)(2,1)S(1)}, u32[]{:S(2)}, u32[]{:S(2)}) async-start(bf16[16,56,128]{2,1,0:T(8,128)(2,1)} %head_product.1), calls=%async_computation.2 | async-start | bytes 458752 | tf_op jit(solution)/shard_map/all_to_all | solution.py:184
  155.7 8.2 %collective-permute-start = (bf16[32,1792]{1,0:T(8,128)(2,1)S(1)}, bf16[32,1792]{1,0:T(8,128)(2,1)S(1)}, u32[]{:S(2)}, u32[]{:S(2)}) collective-permute-start(bf16[32,1792]{1,0:T(8,128)(2,1)S(1)} %get-tuple-element.17), channel_id=1, source_target_pairs={{0,4},{4,0},{1,5},{5,1},{2,6},{6,2},{3,7},{7,3},{8,12},{12,8},{9,1... | collective-permute-start | bytes 344072 | tf_op jit(solution)/shard_map/ppermute | solution.py:169
Sparse Core Ops, SparseCore 0:
  15.5 82.9 all-gather.1
  128.6 26.1 reduce-scatter.1

commit v9 on v8

--- a/solution.py
+++ b/solution.py
@@ -8,7 +8,9 @@
 BF = jnp.bfloat16
 F32 = jnp.float32
 T = ("yh", "x")
-NZ, NYL, NC, NYH, NX = 16, 2, 2, 2, 4
+Z = ("zh", "zl")
+NZH, NZL, NYL, NC, NYH, NX = 2, 8, 2, 2, 2, 4
+NZ = NZH * NZL
 CORES = [(0, 1), (1, 0)]
 
 
@@ -42,6 +44,10 @@
         [total[:, :, 128:], jnp.zeros((*total.shape[:2], 256 - cols), F32)], axis=2
     )
     out_ref[...] = jnp.concatenate([total[:, :, :128], rest], axis=1).astype(BF)
+
+
+def slot(t):
+    return t % NX * NYH + t // NX
 
 
 def pairs_kernel(rows, par_ref, pos_ref, text_hbm, image_ref, out_ref, text_ref, sems):
@@ -82,7 +88,7 @@
             t = row // cols
             end = min((t + 1) * cols, at + 256)
             for low in (0, 1):
-                out_ref[t, pl.ds(low * height + row - t * cols, end - row)] = term[
+                out_ref[slot(t), pl.ds(low * height + row - t * cols, end - row)] = term[
                     row - at : end - at, low * 128 : low * 128 + 128
                 ]
             row = end
@@ -115,7 +121,7 @@
 
 
 def per_device(pooled, texts, head_w, log_scale, bias):
-    z, yl, c = lax.axis_index("z"), lax.axis_index("yl"), lax.axis_index("c")
+    z, yl, c = lax.axis_index(Z), lax.axis_index("yl"), lax.axis_index("c")
     yh, x = lax.axis_index("yh"), lax.axis_index("x")
     rows, width = pooled.shape
     cols = head_w.shape[0]
@@ -126,7 +132,7 @@
         unit_kernel, out_shape=jax.ShapeDtypeStruct(texts.shape, BF), name="unit_texts"
     )(texts)
     text_pair = lax.all_gather(text_unit, "yl", axis=0, tiled=True)
-    text_all = lax.all_gather(text_pair, ("c", "z"), axis=0, tiled=True)
+    text_all = lax.all_gather(text_pair, ("c", *Z), axis=0, tiled=True)
 
     images = gather_t(pooled)
     count = images.shape[0]
@@ -140,7 +146,8 @@
 
     small = width // (NZ * NYL * NC)
     padded = -(-small // 16) * 16
-    parts = images.T.reshape(NZ, NYL * NC, small, count).transpose(1, 0, 2, 3)
+    parts = images.T.reshape(NZH, NZL, NYL * NC, small, count).transpose(2, 1, 0, 3, 4)
+    parts = parts.reshape(NYL * NC, NZ, small, count)
     parts = jnp.pad(parts, ((0, 0), (0, 0), (0, padded - small), (0, 0)))
     parts = lax.all_to_all(parts, ("yl", "c"), split_axis=0, concat_axis=0, tiled=True)
 
@@ -153,7 +160,7 @@
     par = jnp.stack([scale, shift])
     pos = jnp.stack([((c * NZ + z) * NYL + yl) * rows, (x * NYH + yh) * rows]).astype(jnp.int32)
     block = pairs(rows, NYH * NX, par, pos, text_all, embedded)
-    block = lax.all_to_all(block, T, split_axis=0, concat_axis=0, tiled=True)
+    block = lax.all_to_all(block, ("x", "yh"), split_axis=0, concat_axis=0, tiled=True)
     block = scale * jnp.sum(block.astype(F32), axis=0).reshape(2, cols + 16, count // 2)
     row_dots = block[:, cols : cols + 1] + block[:, cols + 1 : cols + 2]
     grad_proj = ((block[:, :cols] - own_unit * row_dots) / norms).astype(BF)
@@ -181,8 +188,7 @@
         ),
         name="head_product",
     )(parts, grad_all)
-    grad_head = lax.all_to_all(grad_head, "z", split_axis=0, concat_axis=0, tiled=True)
-    grad_head, grad_pooled = lax.optimization_barrier((grad_head, grad_pooled))
+    grad_head = lax.all_to_all(grad_head, ("zl", "zh"), split_axis=0, concat_axis=0, tiled=True)
     grad_head = jnp.sum(grad_head.astype(F32), axis=0)
     grad_head = jnp.concatenate(
         [grad_head[:small], grad_head[small:, : cols - 128]], axis=1
@@ -191,8 +197,10 @@
 
 
 def solution(mesh):
-    fine = Mesh(mesh.devices.reshape(NZ, NYL, NC, NYH, NX), ("z", "yl", "c", "yh", "x"))
-    dp = ("z", "yl", "c")
+    fine = Mesh(
+        mesh.devices.reshape(NZH, NZL, NYL, NC, NYH, NX), ("zh", "zl", "yl", "c", "yh", "x")
+    )
+    dp = (*Z, "yl", "c")
     rows = P(dp + T, None)
     return jax.shard_map(
         per_device,

time: 173 us -> 175 us (1.012)
  the two profiles are of different devices: /device:TPU:24 before, /device:TPU:32 now
where the time goes in v9:
time: 175 us
  blocking collectives  89.6 us (51%)
  waiting for transfers between devices  27.6 us (16%)
  starting transfers between devices  16.6 us (9%)
  between operations  15.5 us (9%)
  Pallas kernels  10.2 us (6%)
  local copies, waits for them, and re-layouts  8.39 us (5%)
  other arithmetic  4.75 us (3%)
  matrix products  1.83 us (1%)
    all_gather x2, blocking collectives, gather_t(): lax.all_gather(lax.all_gather(v, 'yh', axis=0, tiled=True), 'x', axis=0,...  29.5 us
    all_gather x2, blocking collectives, gather_t(): lax.all_gather(v, 'yh', axis=0, tiled=True)  23.4 us
    all_to_all x1, blocking collectives, per_device(): lax.all_to_all(block, ('x', 'yh'), split_axis=0, concat_axis=0, tiled=True)  23.2 us
    all_gather x1, waiting for transfers between devices, per_device(): text_all = lax.all_gather(text_pair, ('c', *Z), axis=0, tiled=True)  13.5 us
    reduce_scatter x1, waiting for transfers between devices, per_device(): lax.psum_scatter(grad_pooled, 'x', scatter_dimension=0, tiled=True)  8.29 us
    all_to_all x1, starting transfers between devices, per_device(): lax.all_to_all(grad_head, ('zl', 'zh'), split_axis=0, concat_axis=0, tile...  8.09 us
    pallas_call x1, Pallas kernels, pairs(): pl.pallas_call(lambda *refs: pairs_kernel(rows, *refs), in_specs=[smem, s...  7.31 us
    all_gather x1, blocking collectives, per_device(): text_pair = lax.all_gather(text_unit, 'yl', axis=0, tiled=True)  7.23 us
  transfers between devices with their start and end apart: 5, of which 3 were waited for; matrix products, arithmetic and copies ran while one was open for 7% of the time, Pallas kernels for 1%

profile of v9, /device:TPU:32, one launch (start us, length us, event | category | flops | bytes accessed | tf_op | source)
XLA Modules:
  0.0 174.5 jit_solution(6218483070782469448)
XLA Ops:
  7.2 1.7 unit_texts.1
  9.0 7.2 %all_gather.21 = bf16[64,1792]{1,0:T(8,128)(2,1)} all-gather(bf16[32,1792]{1,0:T(8,128)(2,1)} %unit_texts.1), channel_id=1, replica_groups=mesh['zh'=2,'zl'=8,'yl'=2,'c'=2,'yh'=2,'x'=4] {'yl'}, dimensions={0}, use_global_device_ids=true | all-gather | bytes 344064 | tf_op jit(solution)/shard_map/all_gather | solution.py:134
  16.2 7.2 %all_gather.23 = bf16[64,1792]{1,0:T(8,128)(2,1)S(1)} all-gather(bf16[32,1792]{1,0:T(8,128)(2,1)} %param.5), channel_id=1, replica_groups=mesh['zh'=2,'zl'=8,'yl'=2,'c'=2,'yh'=2,'x'=4] {'yh'}, dimensions={0}, use_global_device_ids=true | all-gather | bytes 344064 | tf_op jit(solution)/shard_map/all_gather | solution.py:24
  23.4 14.9 %all_gather.24 = bf16[256,1792]{1,0:T(8,128)(2,1)S(1)} all-gather(bf16[64,1792]{1,0:T(8,128)(2,1)S(1)} %all_gather.23), channel_id=1, replica_groups=mesh['zh'=2,'zl'=8,'yl'=2,'c'=2,'yh'=2,'x'=4] {'x'}, dimensions={0}, use_global_device_ids=true | all-gather | bytes 1146880 | tf_op jit(solution)/shard_map/all_gather | solution.py:24
  38.3 0.5 copy.11
  38.9 1.2 reshape.38
  40.0 1.3 copy.12
  41.4 1.1 pad.4
  42.5 3.5 %all-to-all-start = ((bf16[4,16,32,256]{3,2,1,0:T(8,128)(2,1)}), bf16[4,16,32,256]{3,2,1,0:T(8,128)(2,1)S(1)}, u32[]{:S(2)}, u32[]{:S(2)}) async-start(bf16[4,16,32,256]{3,2,1,0:T(8,128)(2,1)} %pad.4), calls=%async_computation | async-start | bytes 2097152 | tf_op jit(solution)/shard_map/all_to_all | solution.py:152
  47.4 0.5 convolution_convert_fusion.1
  47.9 16.2 %all_gather.25 = bf16[448,256]{1,0:T(8,128)(2,1)S(1)} all-gather(bf16[224,256]{1,0:T(8,128)(2,1)S(1)} %convolution_convert_fusion.1), channel_id=1, replica_groups=mesh['zh'=2,'zl'=8,'yl'=2,'c'=2,'yh'=2,'x'=4] {'yh'}, dimensions={0}, use_global_device_ids=true | all-gather | bytes 344064 | tf_op jit(solution)/shard_map/all_gather | solution.py:24
  64.1 0.1 pad_add_fusion.refs_1_
  64.2 14.5 %all_gather.26 = bf16[1792,256]{1,0:T(8,128)(2,1)S(1)} all-gather(bf16[448,256]{1,0:T(8,128)(2,1)S(1)} %all_gather.25), channel_id=1, replica_groups=mesh['zh'=2,'zl'=8,'yl'=2,'c'=2,'yh'=2,'x'=4] {'x'}, dimensions={0}, use_global_device_ids=true | all-gather | bytes 1146880 | tf_op jit(solution)/shard_map/all_gather | solution.py:24
  78.7 0.3 multiply_reduce_fusion
  79.0 0.1 pad_maximum_fusion.3.refs_0_
  79.1 1.5 copy.9
  80.6 2.7 %copy.10 = f32[1792,256]{0,1:T(8,128)} copy(f32[1792,256]{1,0:T(8,128)} %bitcast.35) | data formatting | bytes 3670016 | tf_op jit(solution)/shard_map/convert_element_type | solution.py:18
  83.4 1.7 fusion.refs_3_
  85.1 13.5 %all-gather.2.cloned.1.call-done.refs_2_ = bf16[2048,1792]{1,0:T(8,128)(2,1)} async-done(((bf16[64,1792]{1,0:T(8,128)(2,1)}), bf16[2048,1792]{1,0:T(8,128)(2,1)}) %all-gather.2.cloned.1.call-update) | async-done | bytes 7340048 | tf_op jit(solution)/shard_map/all_gather | solution.py:135
  98.6 7.3 %pairs.1 = bf16[8,480,128]{2,1,0:T(8,128)(2,1)S(1)} custom-call(f32[2]{0:T(128)S(1)} %pad_maximum_fusion.3.refs_0_, s32[2]{0:T(128)S(1)} %pad_add_fusion.refs_1_, bf16[2048,1792]{1,0:T(8,128)(2,1)} %all-gather.2.cloned.1.call-done.refs_2_, bf16[256,1792]{1,0:T(8,128)(2,1)S(1)} %fusion.refs_3_), custom_call_target="tpu_custom_call" | custom-call | flops 3758096384 | bytes 9175040 | tf_op jit(solution)/shard_map/pairs/pallas_call | solution.py:107
  105.9 23.2 %all_to_all.15 = bf16[8,480,128]{2,1,0:T(8,128)(2,1)S(1)} all-to-all(bf16[8,480,128]{2,1,0:T(8,128)(2,1)S(1)} %pairs.1), channel_id=1, replica_groups=mesh['zh'=2,'zl'=8,'yl'=2,'c'=2,'yh'=2,'x'=4] {'x','yh'}, dimensions={0} | all-to-all | bytes 1966080 | tf_op jit(solution)/shard_map/all_to_all | solution.py:163
  129.1 0.1 convert_reduce_fusion
  129.4 1.4 convolution_convert_fusion
  130.8 6.3 %all_gather.27.grads_ref = bf16[896,256]{1,0:T(8,128)(2,1)S(1)} all-gather(bf16[224,256]{1,0:T(8,128)(2,1)S(1)} %pad_maximum_fusion), channel_id=1, replica_groups=mesh['zh'=2,'zl'=8,'yl'=2,'c'=2,'yh'=2,'x'=4] {'yl','c'}, dimensions={0}, use_global_device_ids=true | all-gather | bytes 573440 | tf_op jit(solution)/shard_map/all_gather | solution.py:179
  137.1 1.2 head_product.1
  138.3 8.1 %all-to-all-start.2 = ((bf16[16,56,128]{2,1,0:T(8,128)(2,1)}), bf16[16,56,128]{2,1,0:T(8,128)(2,1)S(1)}, u32[]{:S(2)}, u32[]{:S(2)}) async-start(bf16[16,56,128]{2,1,0:T(8,128)(2,1)} %head_product.1), calls=%async_computation.3 | async-start | bytes 458752 | tf_op jit(solution)/shard_map/all_to_all | solution.py:191
  146.3 8.3 %reduce-scatter.2.cloned.1.call-done = bf16[64,1792]{1,0:T(8,128)(2,1)} async-done(((bf16[256,1792]{1,0:T(8,128)(2,1)}), bf16[64,1792]{1,0:T(8,128)(2,1)}) %reduce-scatter.2.cloned.1.call-update) | async-done | bytes 229392 | tf_op jit(solution)/shard_map/reduce_scatter | solution.py:172
  154.6 1.0 broadcast_select_fusion
  155.6 4.9 %collective-permute-start = (bf16[32,1792]{1,0:T(8,128)(2,1)S(1)}, bf16[32,1792]{1,0:T(8,128)(2,1)S(1)}, u32[]{:S(2)}, u32[]{:S(2)}) collective-permute-start(bf16[32,1792]{1,0:T(8,128)(2,1)S(1)} %get-tuple-element.14), channel_id=1, source_target_pairs={{0,4},{4,0},{1,5},{5,1},{2,6},{6,2},{3,7},{7,3},{8,12},{12,8},{9,1... | collective-permute-start | bytes 344072 | tf_op jit(solution)/shard_map/ppermute | solution.py:176
  160.5 5.8 %all-to-all-done.2 = bf16[16,56,128]{2,1,0:T(8,128)(2,1)S(1)} async-done(((bf16[16,56,128]{2,1,0:T(8,128)(2,1)}), bf16[16,56,128]{2,1,0:T(8,128)(2,1)S(1)}, u32[]{:S(2)}, u32[]{:S(2)}) %all-to-all-start.2) | async-done | bytes 229408 | tf_op jit(solution)/shard_map/all_to_all | solution.py:191
  166.4 0.6 pad_maximum_fusion.1
  167.0 0.7 convert_add_fusion
  (21 shorter events, 0.3 us)
Async XLA Ops:
  7.2 40.3 %copy-start = (bf16[224,1792]{1,0:T(8,128)(2,1)S(1)}, bf16[224,1792]{1,0:T(8,128)(2,1)}, u32[]{:S(2)}) copy-start(bf16[224,1792]{1,0:T(8,128)(2,1)} %param.7) | copy-start | bytes 2408452
  7.2 91.4 %all-gather.2.cloned.1.call-start = ((), (), s32[]{:S(2)}) async-start(), calls=%async_computation.4 | async-start | bytes 7569408 | tf_op jit(solution)/shard_map/all_gather | solution.py:135
  42.5 42.6 %all-to-all-start = ((bf16[4,16,32,256]{3,2,1,0:T(8,128)(2,1)}), bf16[4,16,32,256]{3,2,1,0:T(8,128)(2,1)S(1)}, u32[]{:S(2)}, u32[]{:S(2)}) async-start(bf16[4,16,32,256]{3,2,1,0:T(8,128)(2,1)} %pad.4), calls=%async_computation | async-start | bytes 2097152 | tf_op jit(solution)/shard_map/all_to_all | solution.py:152
  46.0 108.6 %reduce-scatter.2.cloned.1.call-start = ((), (), s32[]{:S(2)}) async-start(), calls=%async_computation.5 | async-start | bytes 1146880 | tf_op jit(solution)/shard_map/reduce_scatter | solution.py:172
  138.3 28.0 %all-to-all-start.2 = ((bf16[16,56,128]{2,1,0:T(8,128)(2,1)}), bf16[16,56,128]{2,1,0:T(8,128)(2,1)S(1)}, u32[]{:S(2)}, u32[]{:S(2)}) async-start(bf16[16,56,128]{2,1,0:T(8,128)(2,1)} %head_product.1), calls=%async_computation.3 | async-start | bytes 458752 | tf_op jit(solution)/shard_map/all_to_all | solution.py:191
  155.6 11.4 %collective-permute-start = (bf16[32,1792]{1,0:T(8,128)(2,1)S(1)}, bf16[32,1792]{1,0:T(8,128)(2,1)S(1)}, u32[]{:S(2)}, u32[]{:S(2)}) collective-permute-start(bf16[32,1792]{1,0:T(8,128)(2,1)S(1)} %get-tuple-element.14), channel_id=1, source_target_pairs={{0,4},{4,0},{1,5},{5,1},{2,6},{6,2},{3,7},{7,3},{8,12},{12,8},{9,1... | collective-permute-start | bytes 344072 | tf_op jit(solution)/shard_map/ppermute | solution.py:176
Sparse Core Ops, SparseCore 0:
  16.3 82.2 all-gather.1
  130.9 23.7 reduce-scatter.1
